TPU v7x, 128 devices: a whole 4x4x4 slice. The times are simulated.
128 devices in a mesh: dp: 16 (over z, x_lo, core), tensor: 8 (over x_hi, y).
Axes of the slice: x: 4 (x_hi: 2, x_lo: 2; x = x_hi * 2 + x_lo), y: 4, z: 4, core: 2. Of those that a mesh axis runs over, the one named last changes fastest.
Arguments:
- tokens: bfloat16 [24576, 1536], P(('dp', 'tensor')), may hold values from -24 to 24
- gain_attn: float32 [1536], replicated, may hold values from 0.5 to 1.5
- gain_mlp: float32 [1536], replicated, may hold values from 0.5 to 1.5
- w_query: bfloat16 [1536, 1536], P('dp', 'tensor'), may hold values from -0.15625 to 0.15625
- w_key: bfloat16 [1536, 768], P('dp', 'tensor'), may hold values from -0.15625 to 0.15625
- w_value: bfloat16 [1536, 768], P('dp', 'tensor'), may hold values from -0.15625 to 0.15625
- w_out: bfloat16 [1536, 1536], P(('tensor', 'dp')), may hold values from -1.25 to 1.25
- w_gate: bfloat16 [1536, 4096], P('dp', 'tensor'), may hold values from -0.15625 to 0.15625
- w_up: bfloat16 [1536, 4096], P('dp', 'tensor'), may hold values from -0.15625 to 0.15625
- w_down: bfloat16 [4096, 1536], P(('tensor', 'dp')), may hold values from -0.09375 to 0.09375
- segments: int32 [24576], P('dp'), may hold values from 0 to 24575, as said below
- positions: int32 [24576], P('dp'), may hold values from 0 to 1999, as said below
- cotangent: bfloat16 [24576, 1536], P(('dp', 'tensor')), may hold values from -6 to 6
Outputs:
- result: bfloat16 [24576, 1536], P(('dp', 'tensor'))
- token_grad: bfloat16 [24576, 1536], P(('dp', 'tensor'))
- grad_gain_attn: float32 [1536], replicated
- grad_gain_mlp: float32 [1536], replicated
- grad_query: float32 [1536, 1536], P('dp', 'tensor')
- grad_key: float32 [1536, 768], P('dp', 'tensor')
- grad_value: float32 [1536, 768], P('dp', 'tensor')
- grad_out: float32 [1536, 1536], P(('tensor', 'dp'))
- grad_gate: float32 [1536, 4096], P('dp', 'tensor')
- grad_up: float32 [1536, 4096], P('dp', 'tensor')
- grad_down: float32 [4096, 1536], P(('tensor', 'dp'))
Inputs may be any that keep to these rules, and one draw needn't show every extreme that they name: `segments`: segment labels never fall along the tokens; each run of equal labels is one document of 200 to 2000 tokens (the last one may be cut short), documents run on across sequences, and different documents have different labels. positions counts from 0 at the first token of each document and rises by one along it.
All inputs are finite; a program needn't handle non-finite values.
Results may differ from a plain program's by a relative error of at most 0.025.
Values may be sent and summed in bfloat16 or wider, within the bound.
A program may use at most 128 MiB of HBM per device.

v0:
```python
import math

import jax
import jax.numpy as jnp
from jax import lax
from jax.sharding import PartitionSpec as P

HD = 96
SEQ = 512


EPSILON = 1e-05
ROPE_BASE = 100000.0
MASKED = -1e30


def norm_scale(values):
    return lax.rsqrt(jnp.mean(values * values, axis=-1, keepdims=True) + EPSILON)


def norm_back(upstream, values, inverse, gain):
    scaled = upstream * gain
    inner = jnp.sum(scaled * values, axis=-1, keepdims=True)
    return scaled * inverse - values * inner * (inverse * inverse * inverse) / values.shape[-1]


def rotary_tables(places):
    half_size = HD // 2
    exponent = jnp.arange(half_size, dtype=jnp.float32) * (2.0 / HD)
    frequency = jnp.exp(-math.log(ROPE_BASE) * exponent)
    angles = places.astype(jnp.float32)[:, None] * frequency[None, :]
    return (jnp.cos(angles)[:, None, :], jnp.sin(angles)[:, None, :])


def rotate(values, cosine, sine):
    half_size = values.shape[-1] // 2
    front = values[..., :half_size]
    behind = values[..., half_size:]
    return jnp.concatenate(
        [front * cosine - behind * sine, behind * cosine + front * sine], axis=-1
    )


def unrotate(values, cosine, sine):
    half_size = values.shape[-1] // 2
    front = values[..., :half_size]
    behind = values[..., half_size:]
    return jnp.concatenate(
        [front * cosine + behind * sine, behind * cosine - front * sine], axis=-1
    )


def inner_rows(left, right):
    return lax.dot_general(
        left, right, (((0,), (0,)), ((), ())), preferred_element_type=jnp.float32
    )


def outer_cols(left, right):
    return lax.dot_general(
        left, right, (((1,), (1,)), ((), ())), preferred_element_type=jnp.float32
    )


def shards(
    tokens,
    gain_attn,
    gain_mlp,
    w_query,
    w_key,
    w_value,
    w_out,
    w_gate,
    w_up,
    w_down,
    segments,
    positions,
    cotangent,
):
    own_rows = tokens.shape[0]
    tensor_count = lax.axis_size("tensor")
    group_rows = own_rows * tensor_count
    seq_count = group_rows // SEQ
    query_local = w_query.shape[1] // HD
    kv_local = w_key.shape[1] // HD
    repeat = query_local // kv_local
    scale = HD ** (-0.5)
    query_w, key_w, value_w, out_w = (
        lax.all_gather(w_query, "dp", axis=0, tiled=True),
        lax.all_gather(w_key, "dp", axis=0, tiled=True),
        lax.all_gather(w_value, "dp", axis=0, tiled=True),
        lax.all_gather(w_out, "dp", axis=0, tiled=True),
    )
    gate_w, up_w, down_w = (
        lax.all_gather(w_gate, "dp", axis=0, tiled=True),
        lax.all_gather(w_up, "dp", axis=0, tiled=True),
        lax.all_gather(w_down, "dp", axis=0, tiled=True),
    )
    whole_rows = lax.all_gather(tokens, "tensor", axis=0, tiled=True)
    whole_stream = whole_rows.astype(jnp.float32)
    normed = (whole_stream * norm_scale(whole_stream) * gain_attn).astype(jnp.bfloat16)
    cosine, sine = rotary_tables(positions)
    query_raw = jnp.dot(normed, query_w, preferred_element_type=jnp.float32).reshape(
        group_rows, query_local, HD
    )
    key_raw = jnp.dot(normed, key_w, preferred_element_type=jnp.float32).reshape(
        group_rows, kv_local, HD
    )
    query_rot = rotate(query_raw, cosine, sine).astype(jnp.bfloat16)
    key_rot = rotate(key_raw, cosine, sine).astype(jnp.bfloat16)
    value_low = jnp.dot(normed, value_w, preferred_element_type=jnp.float32).astype(jnp.bfloat16)
    labels = segments.reshape(seq_count, SEQ)
    spots = jnp.arange(SEQ)
    allowed = (labels[:, :, None] == labels[:, None, :]) & (
        spots[None, None, :] <= spots[None, :, None]
    )
    allowed = allowed[:, None, None]
    query_blocks = query_rot.reshape(seq_count, SEQ, kv_local, repeat, HD)
    key_blocks = key_rot.reshape(seq_count, SEQ, kv_local, HD)
    value_blocks = value_low.reshape(seq_count, SEQ, kv_local, HD)
    scores = (
        jnp.einsum(
            "bikrd,bjkd->bkrij", query_blocks, key_blocks, preferred_element_type=jnp.float32
        )
        * scale
    )
    scores = jnp.where(allowed, scores, MASKED)
    highest = jnp.max(scores, axis=-1, keepdims=True)
    weights = jnp.exp(scores - highest)
    row_totals = jnp.sum(weights, axis=-1, keepdims=True)
    log_total = highest + jnp.log(row_totals)
    prob_low = (weights / row_totals).astype(jnp.bfloat16)
    mixed = jnp.einsum(
        "bkrij,bjkd->bikrd", prob_low, value_blocks, preferred_element_type=jnp.float32
    )
    mixed = mixed.astype(jnp.bfloat16).reshape(group_rows, query_local * HD)
    attn_own = lax.psum_scatter(
        jnp.dot(mixed, out_w, preferred_element_type=jnp.float32).astype(jnp.bfloat16),
        "tensor",
        scatter_dimension=0,
        tiled=True,
    ).astype(jnp.float32)
    middle = tokens.astype(jnp.float32) + attn_own
    inverse_two = norm_scale(middle)
    second = (middle * inverse_two * gain_mlp).astype(jnp.bfloat16)
    second_full = lax.all_gather(second, "tensor", axis=0, tiled=True)
    gate = jnp.dot(second_full, gate_w, preferred_element_type=jnp.float32)
    upward = jnp.dot(second_full, up_w, preferred_element_type=jnp.float32)
    sigmoid_gate = jax.nn.sigmoid(gate)
    silu_gate = gate * sigmoid_gate
    hidden = (silu_gate * upward).astype(jnp.bfloat16)
    mlp_own = lax.psum_scatter(
        jnp.dot(hidden, down_w, preferred_element_type=jnp.float32).astype(jnp.bfloat16),
        "tensor",
        scatter_dimension=0,
        tiled=True,
    ).astype(jnp.float32)
    result = (middle + mlp_own).astype(jnp.bfloat16)
    upstream_full = lax.all_gather(cotangent, "tensor", axis=0, tiled=True)
    grad_w_down = inner_rows(hidden, upstream_full)
    grad_hidden = outer_cols(upstream_full, down_w)
    slope = sigmoid_gate * (1.0 + gate * (1.0 - sigmoid_gate))
    grad_gate_act = (grad_hidden * upward * slope).astype(jnp.bfloat16)
    grad_up_act = (grad_hidden * silu_gate).astype(jnp.bfloat16)
    grad_w_gate = inner_rows(second_full, grad_gate_act)
    grad_w_up = inner_rows(second_full, grad_up_act)
    grad_second = lax.psum_scatter(
        (outer_cols(grad_gate_act, gate_w) + outer_cols(grad_up_act, up_w)).astype(jnp.bfloat16),
        "tensor",
        scatter_dimension=0,
        tiled=True,
    ).astype(jnp.float32)
    stream_back = cotangent.astype(jnp.float32) + norm_back(
        grad_second, middle, inverse_two, gain_mlp
    )
    gain_two_part = jnp.sum(grad_second * middle * inverse_two, axis=0)
    grad_attn = lax.all_gather(stream_back.astype(jnp.bfloat16), "tensor", axis=0, tiled=True)
    grad_w_out = inner_rows(mixed, grad_attn)
    grad_mixed = (
        outer_cols(grad_attn, out_w)
        .astype(jnp.bfloat16)
        .reshape(seq_count, SEQ, kv_local, repeat, HD)
    )
    scores_again = (
        jnp.einsum(
            "bikrd,bjkd->bkrij", query_blocks, key_blocks, preferred_element_type=jnp.float32
        )
        * scale
    )
    scores_again = jnp.where(allowed, scores_again, MASKED)
    prob = jnp.exp(scores_again - log_total)
    prob_again = prob.astype(jnp.bfloat16)
    grad_prob = jnp.einsum(
        "bikrd,bjkd->bkrij", grad_mixed, value_blocks, preferred_element_type=jnp.float32
    )
    row_inner = jnp.sum(prob * grad_prob, axis=-1, keepdims=True)
    grad_scores = (prob * (grad_prob - row_inner)).astype(jnp.bfloat16)
    grad_query_rot = (
        jnp.einsum("bkrij,bjkd->bikrd", grad_scores, key_blocks, preferred_element_type=jnp.float32)
        * scale
    )
    grad_key_rot = (
        jnp.einsum(
            "bkrij,bikrd->bjkd", grad_scores, query_blocks, preferred_element_type=jnp.float32
        )
        * scale
    )
    grad_value_act = jnp.einsum(
        "bkrij,bikrd->bjkd", prob_again, grad_mixed, preferred_element_type=jnp.float32
    )
    grad_value_act = grad_value_act.astype(jnp.bfloat16).reshape(group_rows, kv_local * HD)
    grad_query_act = unrotate(grad_query_rot.reshape(group_rows, query_local, HD), cosine, sine)
    grad_query_act = grad_query_act.astype(jnp.bfloat16).reshape(group_rows, query_local * HD)
    grad_key_act = unrotate(grad_key_rot.reshape(group_rows, kv_local, HD), cosine, sine)
    grad_key_act = grad_key_act.astype(jnp.bfloat16).reshape(group_rows, kv_local * HD)
    grad_w_query = inner_rows(normed, grad_query_act)
    grad_w_key = inner_rows(normed, grad_key_act)
    grad_w_value = inner_rows(normed, grad_value_act)
    grad_normed = lax.psum_scatter(
        (
            outer_cols(grad_query_act, query_w)
            + outer_cols(grad_key_act, key_w)
            + outer_cols(grad_value_act, value_w)
        ).astype(jnp.bfloat16),
        "tensor",
        scatter_dimension=0,
        tiled=True,
    ).astype(jnp.float32)
    own_stream = tokens.astype(jnp.float32)
    own_inverse = norm_scale(own_stream)
    token_grad = (stream_back + norm_back(grad_normed, own_stream, own_inverse, gain_attn)).astype(
        jnp.bfloat16
    )
    gain_one_part = jnp.sum(grad_normed * own_stream * own_inverse, axis=0)
    summed_grads = (
        lax.psum_scatter(
            grad_w_query.astype(jnp.bfloat16), "dp", scatter_dimension=0, tiled=True
        ).astype(jnp.float32),
        lax.psum_scatter(
            grad_w_key.astype(jnp.bfloat16), "dp", scatter_dimension=0, tiled=True
        ).astype(jnp.float32),
        lax.psum_scatter(
            grad_w_value.astype(jnp.bfloat16), "dp", scatter_dimension=0, tiled=True
        ).astype(jnp.float32),
        lax.psum_scatter(
            grad_w_out.astype(jnp.bfloat16), "dp", scatter_dimension=0, tiled=True
        ).astype(jnp.float32),
        lax.psum_scatter(
            grad_w_gate.astype(jnp.bfloat16), "dp", scatter_dimension=0, tiled=True
        ).astype(jnp.float32),
        lax.psum_scatter(
            grad_w_up.astype(jnp.bfloat16), "dp", scatter_dimension=0, tiled=True
        ).astype(jnp.float32),
        lax.psum_scatter(
            grad_w_down.astype(jnp.bfloat16), "dp", scatter_dimension=0, tiled=True
        ).astype(jnp.float32),
    )
    gain_grads = lax.psum((gain_one_part, gain_two_part), ("dp", "tensor"))
    return (
        result,
        token_grad,
        gain_grads[0],
        gain_grads[1],
        summed_grads[0],
        summed_grads[1],
        summed_grads[2],
        summed_grads[3],
        summed_grads[4],
        summed_grads[5],
        summed_grads[6],
    )


def solution(mesh):
    placed = (
        P(("dp", "tensor"), None),
        P(),
        P(),
        P("dp", "tensor"),
        P("dp", "tensor"),
        P("dp", "tensor"),
        P(("tensor", "dp"), None),
        P("dp", "tensor"),
        P("dp", "tensor"),
        P(("tensor", "dp"), None),
        P("dp"),
        P("dp"),
        P(("dp", "tensor"), None),
    )
    return jax.shard_map(
        shards,
        mesh=mesh,
        in_specs=placed,
        out_specs=(
            P(("dp", "tensor"), None),
            P(("dp", "tensor"), None),
            P(),
            P(),
            P("dp", "tensor"),
            P("dp", "tensor"),
            P("dp", "tensor"),
            P(("tensor", "dp"), None),
            P("dp", "tensor"),
            P("dp", "tensor"),
            P(("tensor", "dp"), None),
        ),
        check_vma=False,
    )
```

profile of v0, /device:TPU:1, one launch (start us, length us, event | category | flops | bytes accessed | tf_op | source)
XLA Modules:
  0.0 1192.7 jit_solution(2415693068091183719)
XLA Ops:
  10.2 28.1 %all-gather = bf16[16,12,1536]{2,1,0:T(8,128)(2,1)S(1)} all-gather(bf16[1,12,1536]{2,1,0:T(8,128)(2,1)} %bitcast.177), channel_id=1, replica_groups=mesh['dp'=16,'tensor'=8] {'dp'}, dimensions={0}, use_global_device_ids=true | all-gather | bytes 626688 | tf_op jit(solution)/shard_map/all_gather | solution.py:92
  38.6 18.1 %all_gather.35 = bf16[1536,96]{1,0:T(8,128)(2,1)S(1)} all-gather(bf16[96,96]{1,0:T(8,128)(2,1)} %param.17), channel_id=1, replica_groups=mesh['dp'=16,'tensor'=8] {'dp'}, dimensions={0}, use_global_device_ids=true | all-gather | bytes 313344 | tf_op jit(solution)/shard_map/all_gather | solution.py:90
  56.7 22.9 %all_gather.34 = bf16[1536,96]{1,0:T(8,128)(2,1)S(1)} all-gather(bf16[96,96]{1,0:T(8,128)(2,1)S(1)} %copy-done.36), channel_id=1, replica_groups=mesh['dp'=16,'tensor'=8] {'dp'}, dimensions={0}, use_global_device_ids=true | all-gather | bytes 313344 | tf_op jit(solution)/shard_map/all_gather | solution.py:91
  79.5 20.6 %all_gather.36 = bf16[1536,192]{1,0:T(8,128)(2,1)S(1)} all-gather(bf16[96,192]{1,0:T(8,128)(2,1)S(1)} %copy-done.34), channel_id=1, replica_groups=mesh['dp'=16,'tensor'=8] {'dp'}, dimensions={0}, use_global_device_ids=true | all-gather | bytes 626688 | tf_op jit(solution)/shard_map/all_gather | solution.py:89
  100.1 1.5 compare_and_fusion
  102.8 3.5 fusion.1
  107.9 2.1 copy-done
  109.9 1.6 convolution_convert_fusion.10
  112.5 3.9 convolution_bitcast_fusion
  116.4 1.5 fusion.65
  118.2 4.1 fusion.82
  123.4 1.5 fusion.81
  125.8 1.8 copy-done.1
  130.4 3.6 convolution_convert_fusion.1
  134.7 86.0 %reduce-scatter.13.cloned.1.call-done = bf16[192,1536]{1,0:T(8,128)(2,1)} async-done(((bf16[1536,1536]{1,0:T(8,128)(2,1)}), bf16[192,1536]{1,0:T(8,128)(2,1)}) %reduce-scatter.13.cloned.1.call-update) | async-done | bytes 589840 | tf_op jit(solution)/shard_map/reduce_scatter | solution.py:137
  222.1 2.1 multiply_convert_fusion.3
  226.8 72.1 %all-gather.11.cloned.1.call-done = bf16[1536,1536]{1,0:T(8,128)(2,1)} async-done(((bf16[192,1536]{1,0:T(8,128)(2,1)}), bf16[1536,1536]{1,0:T(8,128)(2,1)}) %all-gather.11.cloned.1.call-update) | async-done | bytes 4718608 | tf_op jit(solution)/shard_map/all_gather | solution.py:146
  298.9 7.2 fusion.84
  306.1 26.6 %all-gather.13.cloned.1.call-done = bf16[1536,512]{1,0:T(8,128)(2,1)} async-done(((bf16[96,512]{1,0:T(8,128)(2,1)}), bf16[1536,512]{1,0:T(8,128)(2,1)}) %all-gather.13.cloned.1.call-update) | async-done | bytes 1572880 | tf_op jit(solution)/shard_map/all_gather | solution.py:95
  332.7 7.1 fusion.83
  339.8 28.1 %all-gather.17.cloned.1.call-done = bf16[512,1536]{1,0:T(8,128)(2,1)} async-done(((bf16[32,1536]{1,0:T(8,128)(2,1)}), bf16[512,1536]{1,0:T(8,128)(2,1)}) %all-gather.17.cloned.1.call-update) | async-done | bytes 1572880 | tf_op jit(solution)/shard_map/all_gather | solution.py:97
  367.9 76.8 %all-gather.19.cloned.1.call-done = bf16[1536,1536]{1,0:T(8,128)(2,1)} async-done(((bf16[192,1536]{1,0:T(8,128)(2,1)}), bf16[1536,1536]{1,0:T(8,128)(2,1)}) %all-gather.19.cloned.1.call-update) | async-done | bytes 4718608 | tf_op jit(solution)/shard_map/all_gather | solution.py:159
  444.7 9.8 multiply_convert_fusion
  454.5 2.6 fusion.85
  457.1 4.4 add_convert_fusion
  461.6 85.2 %reduce-scatter.17.cloned.1.call-done = bf16[192,1536]{1,0:T(8,128)(2,1)} async-done(((bf16[1536,1536]{1,0:T(8,128)(2,1)}), bf16[192,1536]{1,0:T(8,128)(2,1)}) %reduce-scatter.17.cloned.1.call-update) | async-done | bytes 589840 | tf_op jit(solution)/shard_map/reduce_scatter | solution.py:167
  546.9 2.2 fusion.43
  549.1 2.4 fusion.80
  551.7 6.6 convolution_convert_fusion.2
  558.4 6.8 convolution_convert_fusion.3
  565.3 6.6 convolution_convert_fusion.4
  572.0 54.5 %all-gather.21.cloned.1.call-done = bf16[1536,1536]{1,0:T(8,128)(2,1)} async-done(((bf16[192,1536]{1,0:T(8,128)(2,1)}), bf16[1536,1536]{1,0:T(8,128)(2,1)}) %all-gather.21.cloned.1.call-update) | async-done | bytes 4718608 | tf_op jit(solution)/shard_map/all_gather | solution.py:177
  626.5 4.8 convolution_convert_fusion.7
  632.7 4.0 fusion.50
  637.1 7.0 fusion.5
  644.2 4.7 fusion.13
  648.9 1.6 copy-done.3
  651.7 2.2 convolution_convert_fusion.8
  655.3 4.7 convolution_convert_fusion.9
  660.0 2.5 fusion.21
  663.3 1.8 reshape.327
  665.1 1.6 add_convert_fusion.2
  667.0 4.7 convolution_convert_fusion.5
  671.7 5.1 fusion.86
  677.0 5.2 convolution_add_fusion.1
  682.2 3.6 fusion.4
  687.3 5.7 convolution_convert_fusion
  694.9 1.6 convert_element_type.200
  696.5 53.4 %reduce-scatter.29.cloned.1.call-done = bf16[96,512]{1,0:T(8,128)(2,1)} async-done(((bf16[1536,512]{1,0:T(8,128)(2,1)}), bf16[96,512]{1,0:T(8,128)(2,1)}) %reduce-scatter.29.cloned.1.call-update) | async-done | bytes 98320 | tf_op jit(solution)/shard_map/reduce_scatter | solution.py:251
  749.9 1.6 convert_element_type.198
  751.5 61.6 %reduce-scatter.27.cloned.1.call-done = bf16[96,512]{1,0:T(8,128)(2,1)} async-done(((bf16[1536,512]{1,0:T(8,128)(2,1)}), bf16[96,512]{1,0:T(8,128)(2,1)}) %reduce-scatter.27.cloned.1.call-update) | async-done | bytes 98320 | tf_op jit(solution)/shard_map/reduce_scatter | solution.py:248
  813.1 1.6 convert_element_type.196
  814.7 3.5 convolution_convert_fusion.6
  818.2 35.2 %fusion = bf16[16,1536]{1,0:T(8,128)(2,1)S(1)} fusion(bf16[192,1536]{1,0:T(8,128)(2,1)S(1)} %convolution_convert_fusion.6), kind=kCustom, calls=%all-reduce-scatter | all-reduce-scatter fusion | flops 393217 | bytes 639488
  856.0 1.9 collective-permute-start
  861.8 13.1 %reduce-scatter.25.cloned.1.call-done = bf16[96,96]{1,0:T(8,128)(2,1)} async-done(((bf16[1536,96]{1,0:T(8,128)(2,1)}), bf16[96,96]{1,0:T(8,128)(2,1)}) %reduce-scatter.25.cloned.1.call-update) | async-done | bytes 18448 | tf_op jit(solution)/shard_map/reduce_scatter | solution.py:242
  876.2 60.4 %reduce-scatter.23.cloned.1.call-done = bf16[96,96]{1,0:T(8,128)(2,1)} async-done(((bf16[1536,96]{1,0:T(8,128)(2,1)}), bf16[96,96]{1,0:T(8,128)(2,1)}) %reduce-scatter.23.cloned.1.call-update) | async-done | bytes 18448 | tf_op jit(solution)/shard_map/reduce_scatter | solution.py:239
  937.9 60.8 %reduce-scatter.21.cloned.1.call-done = bf16[96,192]{1,0:T(8,128)(2,1)} async-done(((bf16[1536,192]{1,0:T(8,128)(2,1)}), bf16[96,192]{1,0:T(8,128)(2,1)}) %reduce-scatter.21.cloned.1.call-update) | async-done | bytes 36880 | tf_op jit(solution)/shard_map/reduce_scatter | solution.py:236
  998.7 1.4 convert_element_type.188
  1000.1 90.8 %reduce-scatter.19.cloned.1.call-done = bf16[192,1536]{1,0:T(8,128)(2,1)} async-done(((bf16[1536,1536]{1,0:T(8,128)(2,1)}), bf16[192,1536]{1,0:T(8,128)(2,1)}) %reduce-scatter.19.cloned.1.call-update) | async-done | bytes 589840 | tf_op jit(solution)/shard_map/reduce_scatter | solution.py:219
  1091.0 1.4 fusion.49
  1092.4 71.9 %all-reduce.2 = (f32[1536]{0:T(1024)}, f32[1536]{0:T(1024)}) all-reduce(f32[1536]{0:T(1024)S(1)} %get-tuple-element.13, f32[1536]{0:T(1024)} %get-tuple-element.11), channel_id=1, replica_groups=mesh['dp'=16,'tensor'=8] {'dp','tensor'}, use_global_device_ids=true, to_apply=%region_13.14 | all-reduce | flops 3072 | bytes 24576 | tf_op jit(solution)/shard_map/psum | solution.py:258
  1164.3 17.4 %reduce-scatter.15.cloned.1.call-done = bf16[192,1536]{1,0:T(8,128)(2,1)} async-done(((bf16[1536,1536]{1,0:T(8,128)(2,1)}), bf16[192,1536]{1,0:T(8,128)(2,1)}) %reduce-scatter.15.cloned.1.call-update) | async-done | bytes 589840 | tf_op jit(solution)/shard_map/reduce_scatter | solution.py:152
  1181.7 3.2 fusion.38
  (179 shorter events, 33.2 us)
Async XLA Ops:
  8.0 48.7 %copy-start.36 = (bf16[96,96]{1,0:T(8,128)(2,1)S(1)}, bf16[96,96]{1,0:T(8,128)(2,1)}, u32[]{:S(2)}) copy-start(bf16[96,96]{1,0:T(8,128)(2,1)} %param.18) | copy-start | bytes 55300
  8.0 71.5 %copy-start.34 = (bf16[96,192]{1,0:T(8,128)(2,1)S(1)}, bf16[96,192]{1,0:T(8,128)(2,1)}, u32[]{:S(2)}) copy-start(bf16[96,192]{1,0:T(8,128)(2,1)} %param.16) | copy-start | bytes 110596
  8.0 94.7 %all-gather.9.cloned.1.call-start = ((), (), s32[]{:S(2)}) async-start(), calls=%async_computation.10 | async-start | bytes 5308416 | tf_op jit(solution)/shard_map/all_gather | solution.py:99
  8.8 211.9 %reduce-scatter.13.cloned.1.call-start = ((), (), s32[]{:S(2)}) async-start(), calls=%async_computation.11 | async-start | bytes 5308416 | tf_op jit(solution)/shard_map/reduce_scatter | solution.py:137
  56.7 55.8 %copy-start.13 = (bf16[1536,96]{1,0:T(8,128)(2,1)}, bf16[1536,96]{1,0:T(8,128)(2,1)S(1)}, u32[]{:S(2)}) copy-start(bf16[1536,96]{1,0:T(8,128)(2,1)S(1)} %all_gather.35) | copy-start | bytes 884740
  79.5 28.3 %copy-start.11 = (bf16[1536,96]{1,0:T(8,128)(2,1)}, bf16[1536,96]{1,0:T(8,128)(2,1)S(1)}, u32[]{:S(2)}) copy-start(bf16[1536,96]{1,0:T(8,128)(2,1)S(1)} %all_gather.34) | copy-start | bytes 884740
  100.1 6.2 copy-start.33
  102.7 19.6 %copy-start.15 = (f32[1536,48]{0,1:T(8,128)}, f32[1536,48]{0,1:T(8,128)S(1)}, u32[]{:S(2)}) copy-start(f32[1536,48]{0,1:T(8,128)S(1)} %get-tuple-element.31) | copy-start | bytes 884740
  102.7 19.6 %copy-start.16 = (f32[1536,48]{0,1:T(8,128)}, f32[1536,48]{0,1:T(8,128)S(1)}, u32[]{:S(2)}) copy-start(f32[1536,48]{0,1:T(8,128)S(1)} %get-tuple-element.32) | copy-start | bytes 884740
  102.8 3.9 copy-start.4
  107.8 2.1 copy-start
  118.0 4.5 copy-start.28
  118.2 4.4 copy-start.30
  124.9 2.7 copy-start.1
  124.9 2.7 copy-start.19
  134.0 86.7 %copy-start.2 = (bf16[192,1536]{1,0:T(8,128)(2,1)S(1)}, bf16[192,1536]{1,0:T(8,128)(2,1)}, u32[]{:S(2)}) copy-start(bf16[192,1536]{1,0:T(8,128)(2,1)} %param.13) | copy-start | bytes 1769476
  134.0 88.0 %copy-start.32 = (f32[1536]{0:T(1024)S(1)}, f32[1536]{0:T(1024)}, u32[]{:S(2)}) copy-start(f32[1536]{0:T(1024)} %param.15) | copy-start | bytes 18436
  134.1 92.7 %all-gather.15.cloned.1.call-start = ((), (), s32[]{:S(2)}) async-start(), calls=%async_computation.14 | async-start | bytes 1671168 | tf_op jit(solution)/shard_map/all_gather | solution.py:96
  134.7 164.2 %all-gather.11.cloned.1.call-start = ((), (), s32[]{:S(2)}) async-start(), calls=%async_computation.12 | async-start | bytes 5308416 | tf_op jit(solution)/shard_map/all_gather | solution.py:146
  222.0 327.0 %copy-start.35 = (f32[192]{0:T(256)}, f32[192]{0:T(256)S(1)}, u32[]{:S(2)}) copy-start(f32[192]{0:T(256)S(1)} %get-tuple-element.36) | copy-start | bytes 2308
  222.1 327.0 %copy-start.38 = (f32[192]{0:T(256)}, f32[192]{0:T(256)S(1)}, u32[]{:S(2)}) copy-start(f32[192]{0:T(256)S(1)} %get-tuple-element.35) | copy-start | bytes 2308
  224.2 108.5 %all-gather.13.cloned.1.call-start = ((), (), s32[]{:S(2)}) async-start(), calls=%async_computation.13 | async-start | bytes 1671168 | tf_op jit(solution)/shard_map/all_gather | solution.py:95
  224.8 143.1 %all-gather.17.cloned.1.call-start = ((), (), s32[]{:S(2)}) async-start(), calls=%async_computation.15 | async-start | bytes 1671168 | tf_op jit(solution)/shard_map/all_gather | solution.py:97
  225.5 219.2 %all-gather.19.cloned.1.call-start = ((), (), s32[]{:S(2)}) async-start(), calls=%async_computation.17 | async-start | bytes 5308416 | tf_op jit(solution)/shard_map/all_gather | solution.py:159
  226.3 320.6 %reduce-scatter.17.cloned.1.call-start = ((), (), s32[]{:S(2)}) async-start(), calls=%async_computation.18 | async-start | bytes 5308416 | tf_op jit(solution)/shard_map/reduce_scatter | solution.py:167
  444.7 9.8 copy-start.42
  454.4 2.7 copy-start.44
  454.4 2.7 copy-start.43
  454.5 2.7 copy-start.41
  461.6 85.3 %copy-start.5 = (bf16[192,1536]{1,0:T(8,128)(2,1)S(1)}, bf16[192,1536]{1,0:T(8,128)(2,1)}, u32[]{:S(2)}) copy-start(bf16[192,1536]{1,0:T(8,128)(2,1)} %reduce-scatter.13.cloned.1.call-done) | copy-start | bytes 1769476
  461.6 87.5 %copy-start.6 = (bf16[192,1536]{1,0:T(8,128)(2,1)S(1)}, bf16[192,1536]{1,0:T(8,128)(2,1)}, u32[]{:S(2)}) copy-start(bf16[192,1536]{1,0:T(8,128)(2,1)} %param.25) | copy-start | bytes 1769476
  461.6 164.9 %all-gather.21.cloned.1.call-start = ((), (), s32[]{:S(2)}) async-start(), calls=%async_computation.19 | async-start | bytes 5308416 | tf_op jit(solution)/shard_map/all_gather | solution.py:177
  549.1 9.3 copy-start.37
  551.5 143.4 %reduce-scatter.31.cloned.1.call-start = ((), (), s32[]{:S(2)}) async-start(), calls=%async_computation.26 | async-start | bytes 1671168 | tf_op jit(solution)/shard_map/reduce_scatter | solution.py:254
  558.4 191.5 %reduce-scatter.29.cloned.1.call-start = ((), (), s32[]{:S(2)}) async-start(), calls=%async_computation.25 | async-start | bytes 1671168 | tf_op jit(solution)/shard_map/reduce_scatter | solution.py:251
  565.2 247.9 %reduce-scatter.27.cloned.1.call-start = ((), (), s32[]{:S(2)}) async-start(), calls=%async_computation.24 | async-start | bytes 1671168 | tf_op jit(solution)/shard_map/reduce_scatter | solution.py:248
  572.0 302.9 %reduce-scatter.25.cloned.1.call-start = ((), (), s32[]{:S(2)}) async-start(), calls=%async_computation.23 | async-start | bytes 417792 | tf_op jit(solution)/shard_map/reduce_scatter | solution.py:242
  632.7 4.4 copy-start.20
  632.7 11.4 slice-start.2
  637.1 14.5 %copy-start.21 = (bf16[12,8,3,512]{3,1,2,0:T(8,128)(2,1)}, bf16[12,8,3,512]{3,1,2,0:T(8,128)(2,1)S(1)}, u32[]{:S(2)}) copy-start(bf16[12,8,3,512]{3,1,2,0:T(8,128)(2,1)S(1)} %copy.84) | copy-start | bytes 884740
  637.1 7.0 slice-start.3
  637.1 14.5 %slice-start = ((s8[4718592]{0:T(1024)(128)(4,1)}), s8[4194304]{0:T(1024)(128)(4,1)S(1)}, s32[]{:S(2)}) async-start(s8[4718592]{0:T(1024)(128)(4,1)} %bitcast.159), calls=%async_computation.27 | async-start | bytes 8388608
  644.2 6.4 copy-start.18
  644.2 7.5 slice-start.1
  655.1 4.8 copy-start.24
  655.1 4.8 copy-start.26
  655.2 4.8 copy-start.29
  655.2 4.8 copy-start.31
  655.2 281.4 %reduce-scatter.23.cloned.1.call-start = ((), (), s32[]{:S(2)}) async-start(), calls=%async_computation.22 | async-start | bytes 417792 | tf_op jit(solution)/shard_map/reduce_scatter | solution.py:239
  666.7 332.0 %reduce-scatter.21.cloned.1.call-start = ((), (), s32[]{:S(2)}) async-start(), calls=%async_computation.21 | async-start | bytes 835584 | tf_op jit(solution)/shard_map/reduce_scatter | solution.py:236
  671.7 5.2 copy-start.14
  671.7 5.2 copy-start.25
  671.7 5.2 copy-start.27
  676.9 5.3 copy-start.12
  676.9 5.3 copy-start.22
  676.9 414.1 %reduce-scatter.19.cloned.1.call-start = ((), (), s32[]{:S(2)}) async-start(), calls=%async_computation.20 | async-start | bytes 5308416 | tf_op jit(solution)/shard_map/reduce_scatter | solution.py:219
  685.9 495.8 %reduce-scatter.15.cloned.1.call-start = ((), (), s32[]{:S(2)}) async-start(), calls=%async_computation.16 | async-start | bytes 5308416 | tf_op jit(solution)/shard_map/reduce_scatter | solution.py:152
  693.0 121.7 %copy-start.10 = (bf16[24,8,3,512]{3,1,2,0:T(8,128)(2,1)S(1)}, bf16[24,8,3,512]{3,1,2,0:T(8,128)(2,1)}, u32[]{:S(2)}) copy-start(bf16[24,8,3,512]{3,1,2,0:T(8,128)(2,1)} %copy-done.9) | copy-start | bytes 1769476
  814.7 367.1 %copy-start.7 = (bf16[192,1536]{1,0:T(8,128)(2,1)S(1)}, bf16[192,1536]{1,0:T(8,128)(2,1)}, u32[]{:S(2)}) copy-start(bf16[192,1536]{1,0:T(8,128)(2,1)} %param.25) | copy-start | bytes 1769476
  814.7 367.1 %copy-start.8 = (bf16[192,1536]{1,0:T(8,128)(2,1)S(1)}, bf16[192,1536]{1,0:T(8,128)(2,1)}, u32[]{:S(2)}) copy-start(bf16[192,1536]{1,0:T(8,128)(2,1)} %reduce-scatter.17.cloned.1.call-done) | copy-start | bytes 1769476
  853.4 7.0 collective-permute-start.2
  854.7 5.7 collective-permute-start.1
  856.0 4.4 collective-permute-start
  857.9 2.5 collective-permute-start.3
  (6 other events, 7.2 us)
Sparse Core Ops, SparseCore 0:
  11.2 83.3 all-gather.8
  134.2 86.4 reduce-scatter.12
  461.7 85.0 reduce-scatter.16
Sparse Core Ops, SparseCore 1:
  136.2 38.6 all-gather.14
  224.3 74.6 all-gather.10
  300.5 32.2 all-gather.12
  334.5 33.3 all-gather.16
  370.2 74.4 all-gather.18
  551.6 74.8 all-gather.20
  628.8 57.6 reduce-scatter.30
  688.8 61.1 reduce-scatter.28
  752.2 60.9 reduce-scatter.26
  816.2 58.6 reduce-scatter.24
  877.6 58.9 reduce-scatter.22
  939.1 59.6 reduce-scatter.20
  1002.5 88.5 reduce-scatter.18
  1094.9 86.8 reduce-scatter.14
where the time goes:
time: 1200 us; the launch traced here: 1190 us
  waiting for transfers between devices  791 us (66%)
  blocking collectives  197 us (16%)
  matrix products  121 us (10%)
  other arithmetic  41.2 us (3%)
  local copies, waits for them, and re-layouts  18.1 us (2%)
  between operations  17.4 us (1%)
    reduce_scatter x1, waiting for transfers between devices, shards(): lax.psum_scatter((outer_cols(grad_query_act, query_w) + outer_cols(grad_k...  90.8 us
    reduce_scatter x1, waiting for transfers between devices, shards(): lax.psum_scatter(jnp.dot(mixed, out_w, preferred_element_type=jnp.float32...  86 us
    reduce_scatter x1, waiting for transfers between devices, shards(): lax.psum_scatter((outer_cols(grad_gate_act, gate_w) + outer_cols(grad_up_...  85.2 us
    all_gather x1, waiting for transfers between devices, shards(): upstream_full = lax.all_gather(cotangent, 'tensor', axis=0, tiled=True)  76.8 us
    all_gather x1, waiting for transfers between devices, shards(): second_full = lax.all_gather(second, 'tensor', axis=0, tiled=True)  72.1 us
    psum x1, blocking collectives, shards(): gain_grads = lax.psum((gain_one_part, gain_two_part), ('dp', 'tensor'))  71.9 us
    reduce_scatter x1, waiting for transfers between devices, shards(): lax.psum_scatter(grad_w_gate.astype(jnp.bfloat16), 'dp', scatter_dimensio...  61.6 us
    reduce_scatter x1, waiting for transfers between devices, shards(): lax.psum_scatter(grad_w_query.astype(jnp.bfloat16), 'dp', scatter_dimensi...  60.8 us
  transfers between devices with their start and end apart: 21, of which 15 were waited for; matrix products, arithmetic and copies ran while one was open for 13% of the time, Pallas kernels for 0%

commit v1 on v0

v1 whole, which is shorter than its diff:
```python
import functools
import math

import jax
import jax.numpy as jnp
from jax import lax
from jax.experimental import pallas as pl
from jax.experimental.pallas import tpu as pltpu
from jax.sharding import PartitionSpec as P

HD = 96
SEQ = 512
D = 1536
OWN = 192
HALF = 768
WIN = 256

EPSILON = 1e-05
ROPE_BASE = 100000.0
MASKED = -1e30
MESH = pl.DeviceIdType.MESH
ANY = pl.BlockSpec(memory_space=pl.ANY)
VMEM = pl.BlockSpec(memory_space=pltpu.VMEM)
BF16 = jnp.bfloat16
F32 = jnp.float32


def place():
    dp = lax.axis_index("dp")
    tensor = lax.axis_index("tensor")
    return (tensor // 4) * 2 + (dp // 2) % 2, tensor % 4, dp // 4, dp % 2


def device(x, y, z, c):
    return (z * 4 + (x % 2) * 2 + c, (x // 2) * 4 + y)


def turn(pos, by):
    return (pos + by + 4) % 4


class Spot:
    def __init__(self):
        x, y, z, c = place()
        self.x, self.y, self.z, self.c = x, y, z, c
        self.high, self.low = x // 2, x % 2
        self.quad = self.low * 2 + c
        self.sibling = device(x, y, z, 1 - c)
        self.partner = device(turn(x, 2), y, z, 1 - c)

    def along(self, axis, by):
        x, y, z, c = self.x, self.y, self.z, self.c
        if axis == "x":
            return device(turn(x, by), y, z, c)
        if axis == "y":
            return device(x, turn(y, by), z, c)
        return device(x, y, turn(z, by), c)

    def me(self, axis):
        return {"x": self.x, "y": self.y, "z": self.z}[axis]

    def in_quad(self, by):
        other = turn(self.quad, by)
        return other, device(self.high * 2 + other // 2, self.y, self.z, other % 2)


def greet(devices):
    barrier = pltpu.get_barrier_semaphore()
    for who in devices:
        pl.semaphore_signal(barrier, inc=1, device_id=who, device_id_type=MESH)
    pl.semaphore_wait(barrier, len(devices))


class Wires:
    def __init__(self, send_sem, recv_sem):
        self.send_sem, self.recv_sem = send_sem, recv_sem
        self.count = 0
        self.sent = []
        self.moved = []

    def send(self, src, dst, who):
        copy = pltpu.make_async_remote_copy(
            src_ref=src,
            dst_ref=dst,
            send_sem=self.send_sem.at[self.count],
            recv_sem=self.recv_sem.at[self.count],
            device_id=who,
            device_id_type=MESH,
        )
        self.count += 1
        copy.start()
        self.sent.append(copy)
        return copy

    def move(self, src, dst):
        copy = pltpu.make_async_copy(src, dst, self.send_sem.at[self.count])
        self.count += 1
        copy.start()
        return copy

    def close(self):
        for copy in self.sent:
            copy.wait_send()


def add_into(dst, *srcs, chunk=16):
    rows = dst.shape[-2]
    chunk = min(chunk, rows)

    def step(i, carry):
        span = pl.ds(pl.multiple_of(i * chunk, chunk), chunk)
        total = srcs[0][..., span, :].astype(F32)
        for src in srcs[1:]:
            total = total + src[..., span, :].astype(F32)
        dst[..., span, :] = total.astype(dst.dtype)
        return carry

    lax.fori_loop(0, rows // chunk, step, 0)


class RingGather:
    def __init__(self, wires, spot, axis, at):
        self.wires, self.at = wires, at
        self.me = spot.me(axis)
        self.next, self.prev = spot.along(axis, 1), spot.along(axis, -1)

    def start(self, own=None):
        own = own or (lambda half: self.at(self.me, half))
        send, at, me = self.wires.send, self.at, self.me
        self.right0 = send(own(0), at(me, 0), self.next)
        self.left1 = send(own(1), at(me, 1), self.prev)
        self.right1 = send(own(1), at(me, 1), self.next)
        self.left0 = send(own(0), at(me, 0), self.prev)

    def forward(self):
        send, at, me = self.wires.send, self.at, self.me
        self.right0.wait_recv()
        before = at(turn(me, -1), 0)
        self.pass0 = send(before, before, self.next)
        self.left1.wait_recv()
        after = at(turn(me, 1), 1)
        self.pass1 = send(after, after, self.prev)

    def near(self):
        self.right1.wait_recv()
        self.left0.wait_recv()

    def far(self):
        self.pass0.wait_recv()
        self.pass1.wait_recv()


class PairGather:
    def __init__(self, wires, spot, axis, out, own, start, size):
        self.wires, self.spot, self.out, self.own = wires, spot, out, own
        self.rows = pl.ds(start, size)
        cut = size // 2

        def half_rows(half):
            return pl.ds(start + half * cut, cut)

        self.half_rows = half_rows
        self.ring = RingGather(
            wires, spot, axis, lambda pos, half: out.at[spot.c, pos, half_rows(half)]
        )
        self.me = spot.me(axis)

    def share(self, pos):
        block = self.out.at[self.spot.c, pos, self.rows]
        return self.wires.send(block, block, self.spot.sibling)

    def start(self):
        self.ring.start(lambda half: self.own.at[self.half_rows(half)])
        mine = self.own.at[self.rows]
        place_of = self.out.at[self.spot.c, self.me, self.rows]
        self.shared = [self.wires.send(mine, place_of, self.spot.sibling)]
        self.kept = self.wires.move(mine, place_of)

    def forward(self):
        self.ring.forward()
        self.ring.near()
        self.shared.append(self.share(turn(self.me, -1)))
        self.shared.append(self.share(turn(self.me, 1)))

    def far(self):
        self.ring.far()
        self.shared.append(self.share(turn(self.me, 2)))

    def finish(self):
        for copy in self.shared:
            copy.wait_recv()
        self.kept.wait()


class PairScatter:
    def __init__(self, wires, spot, axis, part, got, passed, near, start, size):
        self.wires, self.spot = wires, spot
        self.me = spot.me(axis)
        self.next, self.prev = spot.along(axis, 1), spot.along(axis, -1)
        self.part, self.got, self.passed, self.near = part, got, passed, near
        self.start_row, self.size, self.cut = start, size, size // 2
        self.shared = {}

    def rows(self, half=None):
        if half is None:
            return pl.ds(self.start_row, self.size)
        return pl.ds(self.start_row + half * self.cut, self.cut)

    def share(self, by):
        pos = turn(self.me, by)
        self.shared[by] = self.wires.send(
            self.part.at[1 - self.spot.c, pos, self.rows()],
            self.got.at[pos, self.rows()],
            self.spot.sibling,
        )

    def first(self):
        self.shared[2].wait_recv()
        pos = turn(self.me, 2)
        mine = self.got.at[pos, self.rows()]
        add_into(mine, self.part.at[self.spot.c, pos, self.rows()], mine)
        self.pass0 = self.wires.send(
            self.got.at[pos, self.rows(0)], self.passed.at[0, self.rows(0)], self.next
        )
        self.pass1 = self.wires.send(
            self.got.at[pos, self.rows(1)], self.passed.at[1, self.rows(1)], self.prev
        )

    def second(self):
        self.arriving = []
        after, before = turn(self.me, 1), turn(self.me, -1)
        for by, half, who, side in ((1, 1, self.next, 0), (-1, 0, self.prev, 1)):
            pos = turn(self.me, by)
            self.shared[by].wait_recv()
            mine = self.got.at[pos, self.rows(half)]
            add_into(mine, self.part.at[self.spot.c, pos, self.rows(half)], mine)
            self.arriving.append(self.wires.send(mine, self.near.at[side, self.rows(half)], who))
        for pos, half, who, side, arrived in (
            (after, 0, self.next, 0, self.pass0),
            (before, 1, self.prev, 1, self.pass1),
        ):
            arrived.wait_recv()
            mine = self.got.at[pos, self.rows(half)]
            add_into(
                mine,
                self.part.at[self.spot.c, pos, self.rows(half)],
                mine,
                self.passed.at[side, self.rows(half)],
            )
            self.arriving.append(self.wires.send(mine, self.near.at[side, self.rows(half)], who))

    def arrive(self):
        self.shared[0].wait_recv()
        for copy in self.arriving:
            copy.wait_recv()

    def total(self, span):
        return (
            self.part[self.spot.c, self.me, span].astype(F32)
            + self.got[self.me, span].astype(F32)
            + self.near[0, span].astype(F32)
            + self.near[1, span].astype(F32)
        )


class LineScatter:
    def __init__(self, wires, spot, at, work, passed, near, cut):
        self.wires, self.spot, self.at = wires, spot, at
        self.me = spot.z
        self.next, self.prev = spot.along("z", 1), spot.along("z", -1)
        self.work, self.passed, self.near = work, passed, near
        rows = work.shape[-2]
        self.spans = (pl.ds(0, cut), pl.ds(cut, rows - cut))

    def half(self, ref, half):
        return ref.at[:, self.spans[half]]

    def first(self):
        far = self.at(turn(self.me, 2))
        self.pass0 = self.wires.send(self.half(far, 0), self.half(self.passed.at[0], 0), self.next)
        self.pass1 = self.wires.send(self.half(far, 1), self.half(self.passed.at[1], 1), self.prev)
        after, before = self.at(turn(self.me, 1)), self.at(turn(self.me, -1))
        self.arriving = [
            self.wires.send(self.half(after, 1), self.half(self.near.at[0], 1), self.next),
            self.wires.send(self.half(before, 0), self.half(self.near.at[1], 0), self.prev),
        ]

    def second(self):
        after, before = self.at(turn(self.me, 1)), self.at(turn(self.me, -1))
        for src, half, who, side, arrived in (
            (after, 0, self.next, 0, self.pass0),
            (before, 1, self.prev, 1, self.pass1),
        ):
            arrived.wait_recv()
            mine = self.half(self.work.at[side], half)
            add_into(mine, self.half(src, half), self.half(self.passed.at[side], half))
            self.arriving.append(self.wires.send(mine, self.half(self.near.at[side], half), who))

    def finish(self, out):
        for copy in self.arriving:
            copy.wait_recv()
        add_into(out, self.at(self.me), self.near.at[0], self.near.at[1])


def line_scratch(lines, rows, columns):
    shape = (2, lines, rows, columns)
    return [pltpu.VMEM(shape, BF16)] * 3 + [pltpu.VMEM((lines, rows, columns), BF16)]


def norm_scale(values):
    return lax.rsqrt(jnp.mean(values * values, axis=-1, keepdims=True) + EPSILON)


def norm_back(upstream, values, inverse, gain):
    scaled = upstream * gain
    inner = jnp.sum(scaled * values, axis=-1, keepdims=True)
    return scaled * inverse - values * inner * (inverse * inverse * inverse) / values.shape[-1]


def over_rows(start, size, step, chunk=16):
    def body(i, carry):
        step(pl.ds(pl.multiple_of(start + i * chunk, chunk), chunk))
        return carry

    lax.fori_loop(0, size // chunk, body, 0)


def fold(total, values):
    part = values[0:8]
    for first in range(8, values.shape[0], 8):
        part = part + values[first : first + 8]
    total[...] += part


SUBS = ((0, 96), (96, 96))


def gather_kernel(
    tokens, gain, cot, att, gu, dn, marks,
    normed_out, cot_out, att_out, gu_out, dn_out, marks_out,
    own, att_two, send_sem, recv_sem,
):
    spot = Spot()
    wires = Wires(send_sem, recv_sem)
    x, y, z, c = spot.x, spot.y, spot.z, spot.c
    near = [spot.along(a, by) for a in "xyz" for by in (1, -1)]
    greet(
        near
        + [spot.along("x", 2), spot.along("y", 2), spot.sibling, spot.partner]
        + [spot.in_quad(by)[1] for by in (1, 2, 3)]
    )
    att_keep = wires.move(att, att_two.at[0])
    att_swap = wires.send(att, att_two.at[1], spot.partner)
    gu_here = gu_out.at[y, z, pl.ds(pl.multiple_of(spot.quad * 96, 96), 96)]
    gu_kept = wires.move(gu.at[spot.quad], gu_here)
    gu_swap = []
    for by in (1, 2, 3):
        other, who = spot.in_quad(by)
        gu_swap.append(wires.send(gu.at[other], gu_here, who))
    dn_kept = wires.move(dn, dn_out.at[y, z])
    marks_kept = wires.move(marks, marks_out.at[c])
    marks_got = wires.send(marks, marks_out.at[c], spot.sibling)
    cots = [PairGather(wires, spot, "x", cot_out, cot, s, n) for s, n in SUBS]

    def normalise(span):
        rows = tokens[span, :].astype(F32)
        own[span, :] = (rows * norm_scale(rows) * gain[...]).astype(BF16)

    over_rows(0, OWN, normalise)
    rows_y = [PairGather(wires, spot, "y", normed_out, own, s, n) for s, n in SUBS]
    for g in rows_y:
        g.start()
    for g in cots:
        g.start()

    att_keep.wait()
    att_swap.wait_recv()
    slot = spot.low * 2 + spot.high
    mine = att_two.at[jnp.where(spot.high == c, 0, 1)]
    att_here = att_out.at[z, slot]
    att_moved = wires.move(mine, att_here)
    att_side = [wires.send(mine, att_here, spot.along("x", by)) for by in (1, -1, 2)]
    gu_kept.wait()
    dn_kept.wait()
    for copy in gu_swap:
        copy.wait_recv()
    side = []
    for by in (1, -1, 2):
        side.append(wires.send(gu_out.at[y, z], gu_out.at[y, z], spot.along("y", by)))
        side.append(wires.send(dn_out.at[y, z], dn_out.at[y, z], spot.along("y", by)))

    rows_y[0].forward()
    rows_y[1].forward()
    cots[0].forward()
    cots[1].forward()

    att_moved.wait()
    for copy in att_side:
        copy.wait_recv()
    att_line = RingGather(
        wires, spot, "z", lambda pos, h: att_out.at[pos, :, pl.ds((0, 80)[h], (80, 64)[h])]
    )
    att_line.start()
    for copy in side:
        copy.wait_recv()
    gu_line = RingGather(wires, spot, "z", lambda pos, h: gu_out.at[:, pos, pl.ds(h * 192, 192)])
    dn_line = RingGather(wires, spot, "z", lambda pos, h: dn_out.at[:, pos, pl.ds(h * 16, 16)])
    gu_line.start()
    dn_line.start()
    for g in rows_y + cots:
        g.far()
    for line in (att_line, gu_line, dn_line):
        line.forward()
    for g in rows_y + cots:
        g.finish()
    for line in (att_line, gu_line, dn_line):
        line.near()
        line.far()
    marks_kept.wait()
    marks_got.wait_recv()
    wires.close()


def gather_all(tokens, gain, cot, att, gu, dn, marks):
    shapes = (
        jax.ShapeDtypeStruct((2, 4, OWN, D), BF16),
        jax.ShapeDtypeStruct((2, 4, OWN, D), BF16),
        jax.ShapeDtypeStruct((4, 4, 144, 384), BF16),
        jax.ShapeDtypeStruct((4, 4, 384, 256), BF16),
        jax.ShapeDtypeStruct((4, 4, 32, D), BF16),
        jax.ShapeDtypeStruct((2, 2, D), jnp.int32),
    )
    sems = 96
    return pl.pallas_call(
        gather_kernel,
        out_shape=shapes,
        in_specs=[VMEM, VMEM, VMEM, VMEM, VMEM, VMEM, VMEM],
        out_specs=[ANY] * 6,
        scratch_shapes=[
            pltpu.VMEM((OWN, D), BF16),
            pltpu.VMEM((2, 144, 384), BF16),
            pltpu.SemaphoreType.DMA((sems,)),
            pltpu.SemaphoreType.DMA((sems,)),
        ],
        compiler_params=pltpu.CompilerParams(
            collective_id=1, has_side_effects=True, vmem_limit_bytes=48 << 20
        ),
        name="gather_all",
    )(tokens, gain, cot, att, gu, dn, marks)


def scatter_scratch():
    return [
        pltpu.VMEM((4, OWN, D), BF16),
        pltpu.VMEM((2, OWN, D), BF16),
        pltpu.VMEM((2, OWN, D), BF16),
    ]


def run_through(scatters, gathers, use):
    for by in (2, 1, -1, 0):
        for s in scatters:
            s.share(by)
    for s in scatters:
        s.first()
    for s in scatters:
        s.second()
    for s, g in zip(scatters, gathers):
        s.arrive()
        over_rows(s.start_row, s.size, lambda span, s=s: use(span, s.total(span)))
        g.start()
        g.forward()
    for g in gathers:
        g.far()
    for g in gathers:
        g.finish()


def around(spot, axes):
    return [spot.along(a, by) for a in axes for by in (1, -1)] + [spot.sibling]


def forward_kernel(
    part, tokens, gain, middle_out, second_out, own, got, passed, near, send_sem, recv_sem
):
    spot = Spot()
    wires = Wires(send_sem, recv_sem)
    greet(around(spot, "xy"))
    scatters = [
        PairScatter(wires, spot, "y", part, got, passed, near, s, n) for s, n in SUBS
    ]
    gathers = [PairGather(wires, spot, "x", second_out, own, s, n) for s, n in SUBS]

    def use(span, attn):
        middle = tokens[span, :].astype(F32) + attn
        middle_out[span, :] = middle
        own[span, :] = (middle * norm_scale(middle) * gain[...]).astype(BF16)

    run_through(scatters, gathers, use)
    wires.close()


def forward_exchange(part, tokens, gain):
    sems = 64
    return pl.pallas_call(
        forward_kernel,
        out_shape=(
            jax.ShapeDtypeStruct((OWN, D), F32),
            jax.ShapeDtypeStruct((2, 4, OWN, D), BF16),
        ),
        in_specs=[VMEM, VMEM, VMEM],
        out_specs=[VMEM, ANY],
        scratch_shapes=[pltpu.VMEM((OWN, D), BF16)]
        + scatter_scratch()
        + [pltpu.SemaphoreType.DMA((sems,)), pltpu.SemaphoreType.DMA((sems,))],
        compiler_params=pltpu.CompilerParams(
            collective_id=2, has_side_effects=True, vmem_limit_bytes=48 << 20
        ),
        name="forward_exchange",
    )(part, tokens, gain)


def backward_kernel(
    part, cot, middle, gain,
    back_out, grad_out, gain_out,
    own, got, passed, near, total, send_sem, recv_sem,
):
    spot = Spot()
    wires = Wires(send_sem, recv_sem)
    greet(around(spot, "xy"))
    scatters = [
        PairScatter(wires, spot, "x", part, got, passed, near, s, n) for s, n in SUBS
    ]
    gathers = [PairGather(wires, spot, "y", grad_out, own, s, n) for s, n in SUBS]
    total[...] = jnp.zeros_like(total)

    def use(span, grad_second):
        rows = middle[span, :]
        inverse = norm_scale(rows)
        back = cot[span, :].astype(F32) + norm_back(grad_second, rows, inverse, gain[...])
        back_out[span, :] = back
        own[span, :] = back.astype(BF16)
        fold(total, grad_second * rows * inverse)

    run_through(scatters, gathers, use)
    gain_out[...] = jnp.sum(total[...], axis=0, keepdims=True)
    wires.close()


def backward_exchange(part, cot, middle, gain):
    sems = 64
    return pl.pallas_call(
        backward_kernel,
        out_shape=(
            jax.ShapeDtypeStruct((OWN, D), F32),
            jax.ShapeDtypeStruct((2, 4, OWN, D), BF16),
            jax.ShapeDtypeStruct((1, D), F32),
        ),
        in_specs=[VMEM] * 4,
        out_specs=[VMEM, ANY, VMEM],
        scratch_shapes=[pltpu.VMEM((OWN, D), BF16)]
        + scatter_scratch()
        + [
            pltpu.VMEM((8, D), F32),
            pltpu.SemaphoreType.DMA((sems,)),
            pltpu.SemaphoreType.DMA((sems,)),
        ],
        compiler_params=pltpu.CompilerParams(
            collective_id=3, has_side_effects=True, vmem_limit_bytes=48 << 20
        ),
        name="backward_exchange",
    )(part, cot, middle, gain)


def final_kernel(
    normed_part, mlp_part, tokens, gain, back, middle, gain_two, d_att, d_gu, d_dn,
    result_out, token_out, gains_out, att_out, gu_out, dn_out,
    got_y, passed_y, near_y, got_x, passed_x, near_x,
    att_work, att_passed, att_near, att_line,
    gu_work, gu_passed, gu_near, gu_line,
    dn_work, dn_passed, dn_near, dn_line,
    att_in, gu_in, dn_in, att_two, gu_two, gain_c, gain_y, gain_x, gain_z, total,
    send_sem, recv_sem,
):
    spot = Spot()
    wires = Wires(send_sem, recv_sem)
    x, y, z, c = spot.x, spot.y, spot.z, spot.c
    greet(
        around(spot, "xyz")
        + [spot.along(a, 2) for a in "xyz"]
        + [spot.partner]
        + [spot.in_quad(by)[1] for by in (1, 2, 3)]
    )
    rows_y = [
        PairScatter(wires, spot, "y", normed_part, got_y, passed_y, near_y, s, n) for s, n in SUBS
    ]
    rows_x = [
        PairScatter(wires, spot, "x", mlp_part, got_x, passed_x, near_x, s, n) for s, n in SUBS
    ]
    lines = [
        LineScatter(wires, spot, lambda p: d_gu.at[:, p], gu_work, gu_passed, gu_near, 192),
        LineScatter(wires, spot, lambda p: d_dn.at[:, p], dn_work, dn_passed, dn_near, 16),
        LineScatter(wires, spot, lambda p: d_att.at[p], att_work, att_passed, att_near, 80),
    ]
    for line in lines:
        line.first()
    for by in (2, 1, -1, 0):
        for s in rows_y + rows_x:
            s.share(by)
    for s in rows_y + rows_x:
        s.first()
    for s in rows_y + rows_x:
        s.second()
    for line in lines:
        line.second()
    total[...] = jnp.zeros_like(total)

    def token_rows(s):
        def use(span):
            grad = s.total(span)
            rows = tokens[span, :].astype(F32)
            inverse = norm_scale(rows)
            out = back[span, :] + norm_back(grad, rows, inverse, gain[...])
            token_out[span, :] = out.astype(BF16)
            fold(total, grad * rows * inverse)

        return use

    def result_rows(s):
        def use(span):
            result_out[span, :] = (middle[span, :] + s.total(span)).astype(BF16)

        return use

    for s in rows_y:
        s.arrive()
        over_rows(s.start_row, s.size, token_rows(s))
    gain_c[c, 0:1] = jnp.sum(total[...], axis=0, keepdims=True)
    gain_c[c, 1:2] = gain_two[...]
    gain_got = [wires.send(gain_c.at[c], gain_c.at[c], spot.sibling)]
    for s in rows_x:
        s.arrive()
        over_rows(s.start_row, s.size, result_rows(s))

    held = gain_c
    for axis, into in (("y", gain_y), ("x", gain_x), ("z", gain_z), (None, None)):
        for copy in gain_got:
            copy.wait_recv()
        summed = held[0]
        for i in range(1, held.shape[0]):
            summed = summed + held[i]
        if into is None:
            gains_out[...] = summed
            break
        me = spot.me(axis)
        into[me] = summed
        gain_got = [
            wires.send(into.at[me], into.at[me], spot.along(axis, by)) for by in (1, -1, 2)
        ]
        held = into

    lines[0].finish(gu_line)
    gu_got = []
    for by in (1, -1, 2):
        gu_got.append(
            wires.send(gu_line.at[turn(y, by)], gu_in.at[y], spot.along("y", by))
        )
    lines[1].finish(dn_line)
    dn_got = []
    for by in (1, -1, 2):
        dn_got.append(
            wires.send(dn_line.at[turn(y, by)], dn_in.at[y], spot.along("y", by))
        )
    lines[2].finish(att_line)
    att_got = []
    for by in (1, -1, 2):
        far = turn(x, by)
        att_got.append(
            wires.send(
                att_line.at[(far % 2) * 2 + far // 2], att_in.at[x], spot.along("x", by)
            )
        )
    for copy in gu_got:
        copy.wait_recv()
    add_into(gu_line.at[y], gu_line.at[y], *[gu_in.at[turn(y, by)] for by in (1, -1, 2)])
    gu_done = []
    for by in (1, 2, 3):
        other, who = spot.in_quad(by)
        gu_done.append(
            wires.send(
                gu_line.at[y, pl.ds(pl.multiple_of(other * 96, 96), 96)],
                gu_two.at[spot.quad],
                who,
            )
        )
    for copy in att_got:
        copy.wait_recv()
    slot = spot.low * 2 + spot.high
    add_into(att_two.at[0], att_line.at[slot], *[att_in.at[turn(x, by)] for by in (1, -1, 2)])
    att_done = wires.send(att_two.at[0], att_two.at[1], spot.partner)
    for copy in dn_got:
        copy.wait_recv()
    add_into(dn_out, dn_line.at[y], *[dn_in.at[turn(y, by)] for by in (1, -1, 2)])
    own_rows = gu_line.at[y, pl.ds(pl.multiple_of(spot.quad * 96, 96), 96)]
    add_into(gu_out.at[spot.quad], own_rows)
    for copy in gu_done:
        copy.wait_recv()
    for by in (1, 2, 3):
        other = turn(spot.quad, by)
        add_into(gu_out.at[other], gu_two.at[other])
    att_done.wait_recv()
    add_into(att_out, att_two.at[jnp.where(spot.high == c, 0, 1)])
    wires.close()


def final_exchange(normed_part, mlp_part, tokens, gain, back, middle, gain_two, d_att, d_gu, d_dn):
    sems = 128
    return pl.pallas_call(
        final_kernel,
        out_shape=(
            jax.ShapeDtypeStruct((OWN, D), BF16),
            jax.ShapeDtypeStruct((OWN, D), BF16),
            jax.ShapeDtypeStruct((2, D), F32),
            jax.ShapeDtypeStruct((144, 384), F32),
            jax.ShapeDtypeStruct((4, 96, 256), F32),
            jax.ShapeDtypeStruct((32, D), F32),
        ),
        in_specs=[VMEM] * 10,
        out_specs=[VMEM] * 6,
        scratch_shapes=scatter_scratch()
        + scatter_scratch()
        + line_scratch(4, 144, 384)
        + line_scratch(4, 384, 256)
        + line_scratch(4, 32, D)
        + [
            pltpu.VMEM((4, 144, 384), BF16),
            pltpu.VMEM((4, 384, 256), BF16),
            pltpu.VMEM((4, 32, D), BF16),
            pltpu.VMEM((2, 144, 384), BF16),
            pltpu.VMEM((4, 96, 256), BF16),
            pltpu.VMEM((2, 2, D), F32),
            pltpu.VMEM((4, 2, D), F32),
            pltpu.VMEM((4, 2, D), F32),
            pltpu.VMEM((4, 2, D), F32),
            pltpu.VMEM((8, D), F32),
            pltpu.SemaphoreType.DMA((sems,)),
            pltpu.SemaphoreType.DMA((sems,)),
        ],
        compiler_params=pltpu.CompilerParams(
            collective_id=4, has_side_effects=True, vmem_limit_bytes=60 << 20
        ),
        name="final_exchange",
    )(normed_part, mlp_part, tokens, gain, back, middle, gain_two, d_att, d_gu, d_dn)


def rotary_tables(places):
    half_size = HD // 2
    exponent = jnp.arange(half_size, dtype=F32) * (2.0 / HD)
    frequency = jnp.exp(-math.log(ROPE_BASE) * exponent)
    angles = places.astype(F32)[:, None] * frequency[None, :]
    return (jnp.cos(angles)[:, None, :], jnp.sin(angles)[:, None, :])


def rotate(values, cosine, sine):
    half_size = values.shape[-1] // 2
    front = values[..., :half_size]
    behind = values[..., half_size:]
    return jnp.concatenate(
        [front * cosine - behind * sine, behind * cosine + front * sine], axis=-1
    )


def inner_rows(left, right):
    return lax.dot_general(left, right, (((0,), (0,)), ((), ())), preferred_element_type=F32)


def outer_cols(left, right):
    return lax.dot_general(left, right, (((1,), (1,)), ((), ())), preferred_element_type=F32)


def windows(blocks):
    return jnp.stack([blocks[:, i * WIN : i * WIN + SEQ] for i in range(3)], axis=1)


def unwindow(grads):
    none = jnp.zeros_like(grads[:, 0, :WIN])
    low = jnp.concatenate([grads[:, i, :WIN] for i in range(3)] + [none], axis=1)
    high = jnp.concatenate([none] + [grads[:, i, WIN:] for i in range(3)], axis=1)
    return low + high


def shards(
    tokens,
    gain_attn,
    gain_mlp,
    w_query,
    w_key,
    w_value,
    w_out,
    w_gate,
    w_up,
    w_down,
    segments,
    positions,
    cotangent,
):
    scale = HD ** (-0.5)
    rows = 8 * OWN
    half_way = [(t, (t + 4) % 8) for t in range(8)]
    high = lax.axis_index("tensor") // 4

    att = jnp.concatenate(
        [jnp.concatenate([w_query, w_key, w_value], axis=1), w_out.reshape(48, 384)], axis=0
    )

    def by_quad(w):
        return w.reshape(96, 4, 4, 32).transpose(2, 0, 1, 3).reshape(4, 96, 128)

    gu = jnp.concatenate([by_quad(w_gate), by_quad(w_up)], axis=-1)
    marks = jnp.stack([segments, positions])
    normed, cot_full, att_full, gu_full, dn_full, marks_full = gather_all(
        tokens, gain_attn[None], cotangent, att, gu, w_down, marks
    )
    normed = normed.reshape(rows, D)
    cot_full = cot_full.reshape(rows, D)
    qkv_w = att_full[:, :, :96].reshape(D, 384)
    out_w = att_full[:, :, 96:].reshape(OWN, D)
    gu_w = gu_full.reshape(4, D, 256)
    down_w = dn_full.reshape(512, D)

    labels = jnp.pad(marks_full[:, 0], ((0, 0), (WIN, 0)), constant_values=-1)
    labels = lax.dynamic_slice_in_dim(labels, high * HALF, HALF + WIN, axis=1)
    places = lax.dynamic_slice_in_dim(marks_full[:, 1], high * HALF, HALF, axis=1)
    cosine, sine = rotary_tables(places.reshape(rows))

    qkv = jnp.dot(normed, qkv_w, preferred_element_type=F32)
    query = rotate(qkv[:, :192].reshape(rows, 2, HD), cosine, sine).astype(BF16)
    key = rotate(qkv[:, 192:288].reshape(rows, 1, HD), cosine, sine).astype(BF16)
    key = key.reshape(2, HALF, HD)
    value = qkv[:, 288:].astype(BF16).reshape(2, HALF, HD)
    far = lax.ppermute(jnp.concatenate([key, value], axis=-1)[:, SEQ:], "tensor", half_way)
    keys = windows(jnp.concatenate([far[..., :HD], key], axis=1))
    values = windows(jnp.concatenate([far[..., HD:], value], axis=1))

    first = high * HALF + jnp.arange(3)[:, None, None] * WIN
    at_query = first + jnp.arange(WIN)[None, :, None]
    at_key = first - WIN + jnp.arange(SEQ)[None, None, :]
    allowed = (at_key >= 0) & (at_key <= at_query) & (at_key // SEQ == at_query // SEQ)
    mine = labels[:, WIN:].reshape(2, 3, WIN)
    allowed = allowed[None] & (mine[:, :, :, None] == windows(labels)[:, :, None, :])
    allowed = allowed[:, :, None]

    queries = query.reshape(2, 3, WIN, 2, HD)
    scores = jnp.einsum("btird,btjd->btrij", queries, keys, preferred_element_type=F32) * scale
    scores = jnp.where(allowed, scores, MASKED)
    highest = jnp.max(scores, axis=-1, keepdims=True)
    weights = jnp.exp(scores - highest)
    prob = weights / jnp.sum(weights, axis=-1, keepdims=True)
    prob_low = prob.astype(BF16)
    mixed = jnp.einsum("btrij,btjd->btird", prob_low, values, preferred_element_type=F32)
    mixed = mixed.astype(BF16).reshape(rows, 192)
    attn_part = jnp.dot(mixed, out_w, preferred_element_type=F32).astype(BF16)
    middle, second = forward_exchange(attn_part.reshape(2, 4, OWN, D), tokens, gain_mlp[None])
    second = second.reshape(rows, D)

    hidden, gate_acts, d_gu = [], [], []
    grad_second = jnp.zeros((rows, D), F32)
    for i in range(4):
        both = jnp.dot(second, gu_w[i], preferred_element_type=F32)
        gate, upward = both[:, :128], both[:, 128:]
        sigmoid_gate = jax.nn.sigmoid(gate)
        silu_gate = gate * sigmoid_gate
        hidden.append((silu_gate * upward).astype(BF16))
        grad_hidden = outer_cols(cot_full, down_w[i * 128 : (i + 1) * 128])
        slope = sigmoid_gate * (1.0 + gate * (1.0 - sigmoid_gate))
        acts = jnp.concatenate([grad_hidden * upward * slope, grad_hidden * silu_gate], axis=-1)
        acts = acts.astype(BF16)
        grad_second = grad_second + outer_cols(acts, gu_w[i])
        d_gu.append(inner_rows(second, acts).astype(BF16))
    hidden = jnp.concatenate(hidden, axis=-1)
    mlp_part = jnp.dot(hidden, down_w, preferred_element_type=F32).astype(BF16)
    d_dn = inner_rows(hidden, cot_full).astype(BF16)
    d_gu = jnp.stack(d_gu)
    back, grad_attn, gain_two = backward_exchange(
        grad_second.astype(BF16).reshape(2, 4, OWN, D), cotangent, middle, gain_mlp[None]
    )
    grad_attn = grad_attn.reshape(rows, D)

    d_out = inner_rows(mixed, grad_attn).astype(BF16)
    grad_mixed = outer_cols(grad_attn, out_w).astype(BF16).reshape(2, 3, WIN, 2, HD)
    grad_prob = jnp.einsum("btird,btjd->btrij", grad_mixed, values, preferred_element_type=F32)
    row_inner = jnp.sum(prob * grad_prob, axis=-1, keepdims=True)
    grad_scores = (prob * (grad_prob - row_inner)).astype(BF16)
    grad_query = (
        jnp.einsum("btrij,btjd->btird", grad_scores, keys, preferred_element_type=F32) * scale
    )
    grad_keys = (
        jnp.einsum("btrij,btird->btjd", grad_scores, queries, preferred_element_type=F32) * scale
    )
    grad_values = jnp.einsum("btrij,btird->btjd", prob_low, grad_mixed, preferred_element_type=F32)
    grad_kv = unwindow(jnp.concatenate([grad_keys, grad_values], axis=-1))
    far_back = lax.ppermute(grad_kv[:, :WIN].astype(BF16), "tensor", half_way).astype(F32)
    grad_kv = jnp.concatenate(
        [grad_kv[:, WIN : WIN + SEQ], grad_kv[:, WIN + SEQ :] + far_back], axis=1
    ).reshape(rows, 192)
    grad_query_act = rotate(grad_query.reshape(rows, 2, HD), cosine, -sine)
    grad_key_act = rotate(grad_kv[:, :HD].reshape(rows, 1, HD), cosine, -sine)
    acts = jnp.concatenate(
        [grad_query_act.reshape(rows, 192), grad_key_act.reshape(rows, HD), grad_kv[:, HD:]],
        axis=-1,
    ).astype(BF16)
    d_qkv = inner_rows(normed, acts).astype(BF16)
    grad_normed = outer_cols(acts, qkv_w).astype(BF16)

    d_att = jnp.concatenate([d_qkv.reshape(4, 4, 96, 384), d_out.reshape(4, 4, 48, 384)], axis=2)
    result, token_grad, gains, g_att, g_gu, g_dn = final_exchange(
        grad_normed.reshape(2, 4, OWN, D),
        mlp_part.reshape(2, 4, OWN, D),
        tokens,
        gain_attn[None],
        back,
        middle,
        gain_two,
        d_att,
        d_gu.reshape(4, 4, 384, 256),
        d_dn.reshape(4, 4, 32, D),
    )

    def from_quad(g):
        return g.reshape(4, 96, 4, 32).transpose(1, 2, 0, 3).reshape(96, 512)

    return (
        result,
        token_grad,
        gains[0],
        gains[1],
        g_att[:96, :192],
        g_att[:96, 192:288],
        g_att[:96, 288:],
        g_att[96:].reshape(12, D),
        from_quad(g_gu[..., :128]),
        from_quad(g_gu[..., 128:]),
        g_dn,
    )


def solution(mesh):
    placed = (
        P(("dp", "tensor"), None),
        P(),
        P(),
        P("dp", "tensor"),
        P("dp", "tensor"),
        P("dp", "tensor"),
        P(("tensor", "dp"), None),
        P("dp", "tensor"),
        P("dp", "tensor"),
        P(("tensor", "dp"), None),
        P("dp"),
        P("dp"),
        P(("dp", "tensor"), None),
    )
    return jax.shard_map(
        shards,
        mesh=mesh,
        in_specs=placed,
        out_specs=(
            P(("dp", "tensor"), None),
            P(("dp", "tensor"), None),
            P(),
            P(),
            P("dp", "tensor"),
            P("dp", "tensor"),
            P("dp", "tensor"),
            P(("tensor", "dp"), None),
            P("dp", "tensor"),
            P("dp", "tensor"),
            P(("tensor", "dp"), None),
        ),
        check_vma=False,
    )
```

time: 1200 us -> 437 us (0.36)
  waiting for transfers between devices: 791 us -> 0.01 us
  Pallas kernels: 0 us -> 267 us
  blocking collectives: 197 us -> 0 us
  local copies, waits for them, and re-layouts: 18.1 us -> 44.4 us
  matrix products: 121 us -> 96 us
  other arithmetic: 41.2 us -> 18.5 us
  between operations: 17.4 us -> 2.09 us
    reduce_scatter x10 -> x0, waiting for transfers between devices: 529 us -> none  [the longest x1 90.8 us: shards(): lax.psum_scatter((outer_cols(grad_query_act, query_w) + outer_cols(grad_k...]
    pallas_call x0 -> x4, Pallas kernels: none -> 267 us  [the longest x1 86.6 us: final_exchange(): pl.pallas_call(final_kernel, out_shape=(jax.ShapeDtypeStruct((OWN, D), BF...]
    all_gather x7 -> x0, waiting for transfers between devices: 258 us -> none  [the longest x1 76.8 us: shards(): upstream_full = lax.all_gather(cotangent, 'tensor', axis=0, tiled=True)]
    all_gather x4 -> x0, blocking collectives: 89.6 us -> none  [the longest x1 28.1 us: shards(): lax.all_gather(w_out, 'dp', axis=0, tiled=True)]
    psum x1 -> x0, blocking collectives: 71.9 us -> none  [shards(): gain_grads = lax.psum((gain_one_part, gain_two_part), ('dp', 'tensor'))]
    unnamed x1 -> x0, blocking collectives: 35.2 us -> none
    convert_element_type x12 -> x2, other arithmetic: 19.1 us -> 1.5 us  [the longest x1 1.47 us: shards(): grad_scores = (prob * (grad_prob - row_inner)).astype(BF16)]
    dot_general x13 -> x12, matrix products: 50.5 us -> 35.3 us  [the longest x4 9.71 us: shards(): both = jnp.dot(second, gu_w[i], preferred_element_type=F32)]
  transfers between devices with their start and end apart: 21 -> 2, of which waited for: 15 -> 0; matrix products, arithmetic and copies ran while one was open for 13% -> 8% of each run, Pallas kernels for 0% -> 0%
where the time goes in v1:
time: 437 us; the launch traced here: 432 us
  Pallas kernels  267 us (61%)
  matrix products  96 us (22%)
  local copies, waits for them, and re-layouts  44.4 us (10%)
  other arithmetic  18.5 us (4%)
    pallas_call x1, Pallas kernels, final_exchange(): pl.pallas_call(final_kernel, out_shape=(jax.ShapeDtypeStruct((OWN, D), BF...  86.6 us
    pallas_call x1, Pallas kernels, gather_all(): pl.pallas_call(gather_kernel, out_shape=shapes, in_specs=[VMEM, VMEM, VME...  85.2 us
    pallas_call x1, Pallas kernels, forward_exchange(): pl.pallas_call(forward_kernel, out_shape=(jax.ShapeDtypeStruct((OWN, D),...  50.2 us
    pallas_call x1, Pallas kernels, backward_exchange(): pl.pallas_call(backward_kernel, out_shape=(jax.ShapeDtypeStruct((OWN, D),...  45.1 us
    dot_general x10, matrix products, outer_cols(): lax.dot_general(left, right, (((1,), (1,)), ((), ())), preferred_element_...  29 us
    dot_general x7, matrix products, inner_rows(): lax.dot_general(left, right, (((0,), (0,)), ((), ())), preferred_element_...  24.7 us
    unnamed x160, local copies, waits for them, and re-layouts  15.2 us
    dot_general x4, matrix products, shards(): both = jnp.dot(second, gu_w[i], preferred_element_type=F32)  9.71 us
  transfers between devices with their start and end apart: 2, of which 0 were waited for; matrix products, arithmetic and copies ran while one was open for 8% of the time, Pallas kernels for 0%

profile of v1, /device:TPU:1, one launch (start us, length us, event | category | flops | bytes accessed | tf_op | source)
XLA Modules:
  0.0 432.0 jit_solution(12213127846283138291)
XLA Ops:
  1.5 1.0 copy.51
  2.6 1.0 copy.53
  6.1 0.9 pad_maximum_fusion.27.att
  7.1 0.9 copy-done.8
  8.0 85.2 %gather_all.1 = (bf16[2,4,192,1536]{3,2,1,0:T(8,128)(2,1)}, bf16[2,4,192,1536]{3,2,1,0:T(8,128)(2,1)}, bf16[4,4,144,384]{3,2,1,0:T(8,128)(2,1)S(1)}, bf16[4,4,38...) custom-call(bf16[192,1536]{1,0:T(8,128)(2,1)S(1)} %copy-done, ...), custom_call_target="tpu_custom_call" | custom-call | tf_op jit(solution)/shard_map/gather_all/pallas_call | solution.py:434
  93.4 5.8 %fusion.104 = f32[1536,384]{0,1:T(8,128)S(1)} fusion(bf16[1536,1536]{1,0:T(8,128)(2,1)} %bitcast.259, bf16[1536,384]{1,0:T(8,128)(2,1)S(1)} %bitcast.236), kind=kOutput, calls=%fused_computation.213 | convolution fusion | flops 1811939328 | bytes 8257536 | tf_op jit(solution)/shard_map/dot_general | solution.py:836
  99.3 1.4 copy-done.13
  101.4 1.3 fusion.59
  103.6 2.5 collective-permute-start
  106.1 1.9 fusion.64
  109.9 1.1 slice.237
  112.2 0.9 concatenate.95
  115.1 1.3 iota_add_fusion.1
  116.4 1.2 reshape.517
  118.3 3.3 fusion.97
  121.7 1.2 fusion.98
  123.0 0.9 compare_and_fusion.1
  123.9 1.5 compare_and_fusion
  125.5 1.0 fusion.62
  126.6 7.0 %fusion.103 = (f32[2,3,2,256]{3,2,1,0:T(2,128)}, f32[2,3,2,256,512]{3,4,2,1,0:T(8,128)}) fusion(pred[2,3,256,512]{2,3,1,0:T(8,128)(4,1)} %compare_and_fusion, bf16[2,3,256,2,96]{2,4,3,1,0:T(8,128)(2,1)} %copy-done.23, bf16[2,1,512,96]{2,3,1,0:T(8,128)(2,1)} %get-tuple-element.127, bf16[2,1,512,96]{2,3,1,0:T(8,128)(2,1)S(1)} %get-tuple-element.126, ...), kind=kOutput, calls=%fused_computation.212 | convolution fusion | flops 310051328 | bytes 8269824 | tf_op jit(solution)/shard_map/sub | solution.py:857
  133.6 3.4 fusion.21
  137.1 1.5 copy.71
  138.5 1.7 reshape.516
  140.2 4.9 %convolution_convert_fusion.2 = bf16[1536,1536]{1,0:T(8,128)(2,1)} fusion(bf16[1536,192]{0,1:T(8,128)(2,1)S(1)} %reshape.516, bf16[192,1536]{1,0:T(8,128)(2,1)} %reshape.517), kind=kOutput, calls=%fused_computation.7 | convolution fusion | flops 908328960 | bytes 5898240 | tf_op jit(solution)/shard_map/dot_general | solution.py:862
  145.1 50.2 %forward_exchange.1 = (f32[192,1536]{1,0:T(8,128)S(1)}, bf16[2,4,192,1536]{3,2,1,0:T(8,128)(2,1)}) custom-call(bf16[2,4,192,1536]{3,2,1,0:T(8,128)(2,1)} %bitcast.215, bf16[192,1536]{1,0:T(8,128)(2,1)S(1)} %copy-done, f32[1,1536]{1,0:T(1,128)S(1)} %broadcast_in_dim.21.gain), custom_call_target="tpu_custom_call" | custom-call | tf_op jit(solution)/shard_map/forward_exchange/pallas_call | solution.py:505
  195.4 4.2 fusion.105
  199.7 2.5 multiply_convert_fusion.11
  202.2 2.3 convolution_convert_fusion.8
  204.5 1.4 fusion.30
  206.0 1.4 fusion.108
  207.4 2.6 fusion.107
  210.0 1.4 fusion.106
  211.5 2.5 multiply_convert_fusion.9
  214.0 2.3 convolution_convert_fusion.7
  216.3 1.8 convolution_add_fusion.2
  218.1 3.8 multiply_convert_fusion.7
  222.0 4.8 %convolution_convert_fusion.6 = bf16[1536,256]{1,0:T(8,128)(2,1)} fusion(bf16[1536,1536]{1,0:T(8,128)(2,1)} %bitcast.279, bf16[1536,128]{0,1:T(8,128)(2,1)S(1)} %get-tuple-element.71, bf16[1536,128]{0,1:T(8,128)(2,1)S(1)} %get-tuple-element.70), kind=kOutput, calls=%fused_computation.35 | convolution fusion | flops 1209925632 | bytes 6291456 | tf_op jit(solution)/shard_map/dot_general | solution.py:774
  226.8 1.4 convolution_add_fusion.1
  228.3 2.5 multiply_convert_fusion.5
  230.8 4.7 %convolution_convert_fusion.5 = bf16[1536,256]{1,0:T(8,128)(2,1)} fusion(bf16[1536,1536]{1,0:T(8,128)(2,1)} %bitcast.280, bf16[1536,128]{0,1:T(8,128)(2,1)S(1)} %get-tuple-element.69, bf16[1536,128]{0,1:T(8,128)(2,1)S(1)} %get-tuple-element.68), kind=kOutput, calls=%fused_computation.34 | convolution fusion | flops 1209925632 | bytes 6291456 | tf_op jit(solution)/shard_map/dot_general | solution.py:774
  235.5 3.6 fusion.1
  239.1 45.1 %backward_exchange.1 = (f32[192,1536]{1,0:T(8,128)S(1)}, bf16[2,4,192,1536]{3,2,1,0:T(8,128)(2,1)}, f32[1,1536]{1,0:T(1,128)S(1)}) custom-call(bf16[2,4,192,1536]{3,2,1,0:T(8,128)(2,1)} %bitcast.216, bf16[192,1536]{1,0:T(8,128)(2,1)S(1)} %copy-done.2, f32[192,1536]{1,0:T(8,128)S(1)} %get-tuple-element.35.middle, f32[1,1536]{1,0:T(1,128)S(1)} %broadcast_in_dim.21.gain), custom_call_target="tpu_custom_call" | custom-call | tf_op jit(solution)/shard_map/backward_exchange/pallas_call | solution.py:552
  284.3 1.1 copy-done.7
  286.0 5.0 %convolution_convert_fusion.10 = bf16[1536,192]{0,1:T(8,128)(2,1)} fusion(bf16[1536,1536]{1,0:T(8,128)(2,1)} %bitcast.274, bf16[192,1536]{1,0:T(8,128)(2,1)S(1)} %copy-done.20), kind=kOutput, calls=%fused_computation.39 | convolution fusion | flops 906264576 | bytes 5898240 | tf_op jit(solution)/shard_map/dot_general | solution.py:778
  290.9 1.8 reshape.522
  292.8 4.1 fusion.2
  296.9 1.1 fusion.14
  298.1 1.5 fusion.4
  300.6 1.1 fusion.17
  303.3 1.1 convolution_convert_fusion.9
  306.1 1.3 collective-permute-start.1
  307.8 6.7 %convolution_convert_fusion.3 = bf16[512,1536]{1,0:T(8,128)(2,1)} fusion(bf16[1536,1536]{1,0:T(8,128)(2,1)} %bitcast.263, bf16[1536,128]{0,1:T(8,128)(2,1)} %get-tuple-element.83, bf16[1536,128]{0,1:T(8,128)(2,1)} %get-tuple-element.82, bf16[1536,128]{0,1:T(8,128)(2,1)} %get-tuple-element.81, bf16[1536,128]{0,1:T(8,128)(2,1)} %get-tuple-element.80), kind=kOutput, calls=%fused_computation.32 | convolution fusion | flops 2422996992 | bytes 7864320 | tf_op jit(solution)/shard_map/dot_general | solution.py:774
  314.6 4.5 %convolution_convert_fusion = bf16[1536,1536]{1,0:T(8,128)(2,1)} fusion(bf16[512,1536]{1,0:T(8,128)(2,1)S(1)} %bitcast.214, bf16[1536,128]{0,1:T(8,128)(2,1)S(1)} %copy-done.60, bf16[1536,128]{0,1:T(8,128)(2,1)S(1)} %copy-done.59, bf16[1536,128]{0,1:T(8,128)(2,1)S(1)} %copy-done.58, bf16[1536,128]{0,1:T(8,128)(2,1)S(1)} %copy-done.57), kind=kOutput, calls=%fused_computation.5 | convolution fusion | flops 2424569856 | bytes 7864320 | tf_op jit(solution)/shard_map/dot_general | solution.py:881
  319.3 0.9 copy-done.28
  320.7 1.8 pad_maximum_fusion.d_gu
  324.4 1.3 fusion.55
  325.8 2.7 convolution_convert_fusion.4
  328.5 4.4 %convolution_convert_fusion.1 = bf16[1536,1536]{1,0:T(8,128)(2,1)} fusion(bf16[1536,384]{1,0:T(8,128)(2,1)S(1)} %bitcast.237, bf16[1536,96]{0,1:T(8,128)(2,1)S(1)} %slice.419, bf16[1536,96]{0,1:T(8,128)(2,1)S(1)} %maximum_bitcast_fusion.5, bf16[1536,192]{0,1:T(8,128)(2,1)S(1)} %bitcast.248), kind=kOutput, calls=%fused_computation.6 | convolution fusion | flops 1817837568 | bytes 7077888 | tf_op jit(solution)/shard_map/dot_general | solution.py:778
  332.9 1.4 pad_maximum_fusion.1.d_att
  334.3 86.6 %final_exchange.1 = (bf16[192,1536]{1,0:T(8,128)(2,1)}, bf16[192,1536]{1,0:T(8,128)(2,1)}, f32[2,1536]{1,0:T(2,128)}, f32[144,384]{1,0:T(8,128)}, f32[4,96,256]{2,1,0:T(8,128)}, /*index=5*/f32[32,1536]{1,0:T(8,128)}) custom-call(bf16[2,4,192,1536]{3,2,1,0:T(8,128)(2,1)} %bitcast.223, bf16[2,4,192,1536]{3,2,1,0:T(8,128)(2,1)} %bitcast.222, ...), custom_call_target="tpu_custom_call" | custom-call | tf_op jit(solution)/shard_map/final_exchange/pallas_call | solution.py:718
  421.0 1.0 slice.276
  421.9 1.7 fusion.100
  423.6 1.5 slice.273
  425.2 1.1 fusion.99
  (224 shorter events, 24.4 us)
Async XLA Ops:
  0.6 6.4 %copy-start = (bf16[192,1536]{1,0:T(8,128)(2,1)S(1)}, bf16[192,1536]{1,0:T(8,128)(2,1)}, u32[]{:S(2)}) copy-start(bf16[192,1536]{1,0:T(8,128)(2,1)} %tokens.5) | copy-start | bytes 1769476
  0.7 6.4 %copy-start.2 = (bf16[192,1536]{1,0:T(8,128)(2,1)S(1)}, bf16[192,1536]{1,0:T(8,128)(2,1)}, u32[]{:S(2)}) copy-start(bf16[192,1536]{1,0:T(8,128)(2,1)} %cot.3) | copy-start | bytes 1769476
  0.7 105.4 %copy-start.55 = (f32[48]{0:T(128)}, f32[48]{0:T(128)S(1)}, u32[]{:S(2)}) copy-start(f32[48]{0:T(128)S(1)} %multiply_exponential_fusion) | copy-start | bytes 580
  1.5 91.9 %copy-start.9 = (f32[1,1536]{1,0:T(1,128)}, f32[1,1536]{1,0:T(1,128)S(1)}, u32[]{:S(2)}) copy-start(f32[1,1536]{1,0:T(1,128)S(1)} %broadcast_in_dim.14.gain) | copy-start | bytes 18436
  93.2 6.0 %copy-start.3 = (bf16[4,4,144,384]{3,2,1,0:T(8,128)(2,1)}, bf16[4,4,144,384]{3,2,1,0:T(8,128)(2,1)S(1)}, u32[]{:S(2)}) copy-start(bf16[4,4,144,384]{3,2,1,0:T(8,128)(2,1)S(1)} %get-tuple-element.29) | copy-start | bytes 5308420
  93.2 6.0 %copy-start.4 = (bf16[4,4,32,1536]{3,2,1,0:T(8,128)(2,1)}, bf16[4,4,32,1536]{3,2,1,0:T(8,128)(2,1)S(1)}, u32[]{:S(2)}) copy-start(bf16[4,4,32,1536]{3,2,1,0:T(8,128)(2,1)S(1)} %get-tuple-element.32) | copy-start | bytes 4718596
  93.4 5.9 %copy-start.26 = (bf16[4,4,96,384]{3,2,1,0:T(8,128)(2,1)}, bf16[4,4,96,384]{3,2,1,0:T(8,128)(2,1)S(1)}, u32[]{:S(2)}) copy-start(bf16[4,4,96,384]{3,2,1,0:T(8,128)(2,1)S(1)} %slice.212) | copy-start | bytes 3538948
  99.3 1.4 copy-start.13
  103.6 7.4 %slice-start.3 = ((f32[1536,384]{0,1:T(8,128)}), f32[1536,192]{0,1:T(8,128)S(1)}, s32[]{:S(2)}) async-start(f32[1536,384]{0,1:T(8,128)} %copy-done.13), calls=%async_computation.3 | async-start | bytes 2359296 | tf_op jit(solution)/shard_map/slice | solution.py:837
  103.6 21.9 %collective-permute-start = (bf16[2,256,192]{1,2,0:T(8,128)(2,1)}, bf16[2,256,192]{1,2,0:T(8,128)(2,1)S(1)}, u32[]{:S(2)}, u32[]{:S(2)}) collective-permute-start(bf16[2,256,192]{1,2,0:T(8,128)(2,1)} %pad_maximum_fusion.24), channel_id=1, source_target_pairs={{0,4},{1,5},{2,6},{3,7},{4,0},{5,1},{6,2},{7,3},{8,12},{9,13},{10,... | collective-permute-start | bytes 589832 | tf_op jit(solution)/shard_map/ppermute | solution.py:841
  108.0 3.2 copy-start.18
  118.3 3.4 copy-start.5
  121.7 2.2 copy-start.46
  121.7 2.2 copy-start.47
  121.7 3.7 copy-start.21
  121.7 3.7 copy-start.22
  126.6 7.0 %copy-start.41 = (bf16[2,1,512,96]{2,3,1,0:T(8,128)(2,1)S(1)}, bf16[2,1,512,96]{2,3,1,0:T(8,128)(2,1)}, u32[]{:S(2)}) copy-start(bf16[2,1,512,96]{2,3,1,0:T(8,128)(2,1)} %get-tuple-element.97) | copy-start | bytes 589828
  126.6 7.0 %copy-start.43 = (bf16[2,1,512,96]{2,3,1,0:T(8,128)(2,1)S(1)}, bf16[2,1,512,96]{2,3,1,0:T(8,128)(2,1)}, u32[]{:S(2)}) copy-start(bf16[2,1,512,96]{2,3,1,0:T(8,128)(2,1)} %get-tuple-element.98) | copy-start | bytes 589828
  126.6 7.0 %copy-start.45 = (bf16[2,1,512,96]{2,3,1,0:T(8,128)(2,1)S(1)}, bf16[2,1,512,96]{2,3,1,0:T(8,128)(2,1)}, u32[]{:S(2)}) copy-start(bf16[2,1,512,96]{2,3,1,0:T(8,128)(2,1)} %get-tuple-element.99) | copy-start | bytes 589828
  140.2 4.9 %copy-start.14 = (bf16[1536,192]{0,1:T(8,128)(2,1)}, bf16[1536,192]{0,1:T(8,128)(2,1)S(1)}, u32[]{:S(2)}) copy-start(bf16[1536,192]{0,1:T(8,128)(2,1)S(1)} %reshape.516) | copy-start | bytes 1769476
  145.1 50.2 %copy-start.16 = (bf16[1,4,384,256]{3,2,1,0:T(8,128)(2,1)S(1)}, bf16[1,4,384,256]{3,2,1,0:T(8,128)(2,1)}, u32[]{:S(2)}) copy-start(bf16[1,4,384,256]{3,2,1,0:T(8,128)(2,1)} %get-tuple-element.61) | copy-start | bytes 2359300
  145.1 54.5 %slice-start.6 = ((s8[4718592]{0:T(1024)(128)(4,1)}), s8[4194304]{0:T(1024)(128)(4,1)S(1)}, s32[]{:S(2)}) async-start(s8[4718592]{0:T(1024)(128)(4,1)} %bitcast.264), calls=%async_computation.6 | async-start | bytes 8388608
  195.4 43.8 %copy-start.1 = (f32[192,1536]{1,0:T(8,128)}, f32[192,1536]{1,0:T(8,128)S(1)}, u32[]{:S(2)}) copy-start(f32[192,1536]{1,0:T(8,128)S(1)} %get-tuple-element.35.middle) | copy-start | bytes 3538948
  195.4 4.3 copy-start.39
  195.4 4.3 slice-start.7
  195.4 6.8 %slice-start.14 = ((s8[4718592]{0:T(1024)(128)(4,1)}), s8[4194304]{0:T(1024)(128)(4,1)S(1)}, s32[]{:S(2)}) async-start(s8[4718592]{0:T(1024)(128)(4,1)} %bitcast.281), calls=%async_computation.14 | async-start | bytes 8388608
  199.7 2.5 slice-start.15
  204.5 1.4 copy-start.17
  210.0 1.4 copy-start.38
  214.0 4.1 slice-start.8
  216.3 1.8 copy-start.37
  216.3 1.8 slice-start.9
  222.0 6.3 %slice-start.10 = ((s8[4718592]{0:T(1024)(128)(4,1)}), s8[4194304]{0:T(1024)(128)(4,1)S(1)}, s32[]{:S(2)}) async-start(s8[4718592]{0:T(1024)(128)(4,1)} %bitcast.271), calls=%async_computation.10 | async-start | bytes 8388608
  226.8 1.5 copy-start.36
  226.8 1.5 slice-start.11
  239.1 46.8 %copy-start.20 = (bf16[192,1536]{1,0:T(8,128)(2,1)S(1)}, bf16[192,1536]{1,0:T(8,128)(2,1)}, u32[]{:S(2)}) copy-start(bf16[192,1536]{1,0:T(8,128)(2,1)} %reshape.517) | copy-start | bytes 1769476
  285.9 6.8 %copy-start.42 = (bf16[2,1,512,96]{2,3,1,0:T(8,128)(2,1)S(1)}, bf16[2,1,512,96]{2,3,1,0:T(8,128)(2,1)}, u32[]{:S(2)}) copy-start(bf16[2,1,512,96]{2,3,1,0:T(8,128)(2,1)} %get-tuple-element.97) | copy-start | bytes 589828
  285.9 6.8 %copy-start.44 = (bf16[2,1,512,96]{2,3,1,0:T(8,128)(2,1)S(1)}, bf16[2,1,512,96]{2,3,1,0:T(8,128)(2,1)}, u32[]{:S(2)}) copy-start(bf16[2,1,512,96]{2,3,1,0:T(8,128)(2,1)} %get-tuple-element.98) | copy-start | bytes 589828
  285.9 6.8 %copy-start.52 = (f32[2,3,2,256]{3,2,1,0:T(2,128)S(1)}, f32[2,3,2,256]{3,2,1,0:T(2,128)}, u32[]{:S(2)}) copy-start(f32[2,3,2,256]{3,2,1,0:T(2,128)} %get-tuple-element.120) | copy-start | bytes 36868
  285.9 11.0 %slice-start = ((s8[6291456]{0:T(1024)(128)(4,1)}), s8[2097152]{0:T(1024)(128)(4,1)S(1)}, s32[]{:S(2)}) async-start(s8[6291456]{0:T(1024)(128)(4,1)} %bitcast.217), calls=%async_computation | async-start | bytes 4194304
  292.8 4.2 slice-start.1
  298.1 1.5 copy-start.32
  298.1 1.5 copy-start.33
  300.6 2.2 slice-start.12
  301.7 1.4 slice-start.13
  302.3 2.2 copy-start.11
  306.1 16.5 %collective-permute-start.1 = (bf16[2,256,192]{1,2,0:T(8,128)(2,1)S(1)}, bf16[2,256,192]{1,2,0:T(8,128)(2,1)S(1)}, u32[]{:S(2)}, u32[]{:S(2)}) collective-permute-start(bf16[2,256,192]{1,2,0:T(8,128)(2,1)S(1)} %slice.421), channel_id=1, source_target_pairs={{0,4},{1,5},{2,6},{3,7},{4,0},{5,1},{6,2},{7,3},{8,12},{9,13},{10,... | collective-permute-start | bytes 589832 | tf_op jit(solution)/shard_map/ppermute | solution.py:902
  307.7 6.8 %copy-start.6 = (bf16[4,4,32,1536]{3,2,1,0:T(8,128)(2,1)S(1)}, bf16[4,4,32,1536]{3,2,1,0:T(8,128)(2,1)}, u32[]{:S(2)}) copy-start(bf16[4,4,32,1536]{3,2,1,0:T(8,128)(2,1)} %copy-done.4) | copy-start | bytes 4718596
  307.7 6.8 %copy-start.57 = (bf16[1536,128]{0,1:T(8,128)(2,1)S(1)}, bf16[1536,128]{0,1:T(8,128)(2,1)}, u32[]{:S(2)}) copy-start(bf16[1536,128]{0,1:T(8,128)(2,1)} %get-tuple-element.80) | copy-start | bytes 1179652
  307.8 6.8 %copy-start.58 = (bf16[1536,128]{0,1:T(8,128)(2,1)S(1)}, bf16[1536,128]{0,1:T(8,128)(2,1)}, u32[]{:S(2)}) copy-start(bf16[1536,128]{0,1:T(8,128)(2,1)} %get-tuple-element.81) | copy-start | bytes 1179652
  307.8 6.8 %copy-start.59 = (bf16[1536,128]{0,1:T(8,128)(2,1)S(1)}, bf16[1536,128]{0,1:T(8,128)(2,1)}, u32[]{:S(2)}) copy-start(bf16[1536,128]{0,1:T(8,128)(2,1)} %get-tuple-element.82) | copy-start | bytes 1179652
  307.8 6.8 %copy-start.60 = (bf16[1536,128]{0,1:T(8,128)(2,1)S(1)}, bf16[1536,128]{0,1:T(8,128)(2,1)}, u32[]{:S(2)}) copy-start(bf16[1536,128]{0,1:T(8,128)(2,1)} %get-tuple-element.83) | copy-start | bytes 1179652
  307.8 17.9 %slice-start.4 = ((s8[4718592]{0:T(1024)(128)(4,1)}), s8[4194304]{0:T(1024)(128)(4,1)S(1)}, s32[]{:S(2)}) async-start(s8[4718592]{0:T(1024)(128)(4,1)} %bitcast.260), calls=%async_computation.4 | async-start | bytes 8388608
  314.6 4.5 %copy-start.19 = (f32[1536,48]{0,1:T(8,128)S(1)}, f32[1536,48]{0,1:T(8,128)}, u32[]{:S(2)}) copy-start(f32[1536,48]{0,1:T(8,128)} %copy-done.18) | copy-start | bytes 884740
  314.6 4.5 %copy-start.25 = (f32[1536,48]{0,1:T(8,128)S(1)}, f32[1536,48]{0,1:T(8,128)}, u32[]{:S(2)}) copy-start(f32[1536,48]{0,1:T(8,128)} %get-tuple-element.113) | copy-start | bytes 884740
  314.6 4.7 %copy-start.31 = (bf16[1536,256]{1,0:T(8,128)(2,1)S(1)}, bf16[1536,256]{1,0:T(8,128)(2,1)}, u32[]{:S(2)}) copy-start(bf16[1536,256]{1,0:T(8,128)(2,1)} %convolution_convert_fusion.5) | copy-start | bytes 2359300
  314.6 11.1 %slice-start.5 = ((s8[4718592]{0:T(1024)(128)(4,1)}), s8[524288]{0:T(1024)(128)(4,1)S(1)}, s32[]{:S(2)}) async-start(s8[4718592]{0:T(1024)(128)(4,1)} %bitcast.260), calls=%async_computation.5 | async-start | bytes 1048576
  319.1 1.6 copy-start.30
  320.7 2.0 copy-start.12
  325.7 2.7 copy-start.27
  421.0 7.9 %copy-start.53 = (f32[2,1536]{1,0:T(2,128)S(1)}, f32[2,1536]{1,0:T(2,128)}, u32[]{:S(2)}) copy-start(f32[2,1536]{1,0:T(2,128)} %get-tuple-element.41) | copy-start | bytes 36868
  421.0 8.6 %copy-start.35 = (bf16[192,1536]{1,0:T(8,128)(2,1)S(1)}, bf16[192,1536]{1,0:T(8,128)(2,1)}, u32[]{:S(2)}) copy-start(bf16[192,1536]{1,0:T(8,128)(2,1)} %get-tuple-element.140) | copy-start | bytes 1769476
  425.2 5.2 %copy-start.34 = (bf16[192,1536]{1,0:T(8,128)(2,1)S(1)}, bf16[192,1536]{1,0:T(8,128)(2,1)}, u32[]{:S(2)}) copy-start(bf16[192,1536]{1,0:T(8,128)(2,1)} %get-tuple-element.141) | copy-start | bytes 1769476
  426.5 4.7 %copy-start.40 = (f32[32,1536]{1,0:T(8,128)S(1)}, f32[32,1536]{1,0:T(8,128)}, u32[]{:S(2)}) copy-start(f32[32,1536]{1,0:T(8,128)} %get-tuple-element.150) | copy-start | bytes 589828
  (15 other events, 16.8 us)
